TPU v7x, 32 devices: a whole 2x2x4 slice. The times are simulated.
32 devices in a mesh: dp: 8 (over z, x), tensor: 4 (over y, core).
Axes of the slice: x: 2, y: 2, z: 4, core: 2. Of those that a mesh axis runs over, the one named last changes fastest.
Arguments:
- tokens: bfloat16 [24576, 768], P(('dp', 'tensor')), may hold values from -6 to 6
- timesteps: int32 [192], P(('dp', 'tensor')), may hold values from 0 to 1999
- lengths: int32 [192], P('dp'), may hold values from 64 to 128, as said below
- time_inner: bfloat16 [128, 512], replicated, may hold values from -0.5 to 0.5
- time_ibias: bfloat16 [512], replicated, may hold values from -3 to 3
- time_outer: bfloat16 [512, 768], replicated, may hold values from -0.25 to 0.25
- time_obias: bfloat16 [768], replicated, may hold values from -1.75 to 1.75
- qkv_weight: bfloat16 [768, 3, 768], P(None, None, 'tensor'), may hold values from -0.21875 to 0.21875
- qv_bias: bfloat16 [2, 768], P(None, 'tensor'), may hold values from -3 to 3
- out_weight: bfloat16 [768, 768], P('tensor'), may hold values from -0.625 to 0.625
- out_bias: bfloat16 [768], replicated, may hold values from -1.75 to 1.75
- gain_first: bfloat16 [768], replicated, may hold values from 0.25 to 1.75
- shift_first: bfloat16 [768], replicated, may hold values from -1.75 to 1.75
- up_weight: bfloat16 [3072, 768], P('tensor'), may hold values from -0.21875 to 0.21875
- up_bias: bfloat16 [3072], P('tensor'), may hold values from -3 to 3
- down_weight: bfloat16 [3072, 768], P('tensor'), may hold values from -0.109375 to 0.109375
- down_bias: bfloat16 [768], replicated, may hold values from -1.75 to 1.75
- gain_second: bfloat16 [768], replicated, may hold values from 0.25 to 1.75
- shift_second: bfloat16 [768], replicated, may hold values from -1.75 to 1.75
- cotangent: bfloat16 [24576, 768], P(('dp', 'tensor')), may hold values from -6 to 6
Outputs:
- layer_out: bfloat16 [24576, 768], P(('dp', 'tensor'))
- grad_tokens: float32 [24576, 768], P(('dp', 'tensor'))
- grad_tinner: float32 [128, 512], replicated
- grad_tibias: float32 [512], replicated
- grad_touter: float32 [512, 768], replicated
- grad_tobias: float32 [768], replicated
- grad_qkv: float32 [768, 3, 768], P(None, None, 'tensor')
- grad_qvbias: float32 [2, 768], P(None, 'tensor')
- grad_wout: float32 [768, 768], P('tensor')
- grad_bout: float32 [768], replicated
- grad_gfirst: float32 [768], replicated
- grad_sfirst: float32 [768], replicated
- grad_wup: float32 [3072, 768], P('tensor')
- grad_bup: float32 [3072], P('tensor')
- grad_wdown: float32 [3072, 768], P('tensor')
- grad_bdown: float32 [768], replicated
- grad_gsecond: float32 [768], replicated
- grad_ssecond: float32 [768], replicated
Inputs may be any that keep to these rules, and one draw needn't show every extreme that they name: `lengths`: each sequence has 64 or 128 tokens that are not padding; some sequence has 128.
All inputs are finite; a program needn't handle non-finite values.
Results may differ from a plain program's by a relative error of at most 0.018.
Values may be sent and summed in bfloat16 or wider, within the bound.
No kernel may reach another device: no remote copies, remote signals or barrier semaphores. Data moves between devices by JAX's collectives and lax.ppermute only.
A program may use at most 128 MiB of HBM per device.

v0:
```python
import math

import jax
import jax.numpy as jnp
from jax import lax
from jax.sharding import PartitionSpec as P

L = 128
HEAD_DIM = 64


eps_norm = 1e-05
normal_dims = ((1,), (0,))
trans_right = ((1,), (1,))
trans_left = ((0,), (0,))


def exact(left, right, dims):
    return lax.dot_general(
        left,
        right,
        (dims, ((), ())),
        precision=lax.Precision.HIGHEST,
        preferred_element_type=jnp.float32,
    )


def direct(left, right, dims):
    return lax.dot_general(left, right, (dims, ((), ())), preferred_element_type=jnp.float32)


def gelu_exact(value):
    return jax.nn.gelu(value, approximate=False)


def norm_forward(value, gain, shift):
    centre = jnp.mean(value, axis=-1, keepdims=True)
    spread = jnp.mean(jnp.square(value - centre), axis=-1, keepdims=True)
    scaled = lax.rsqrt(spread + eps_norm)
    unit = (value - centre) * scaled
    return (unit * gain + shift, unit, scaled)


def norm_backward(upper, unit, scaled, gain):
    inner = upper * gain
    lower = scaled * (
        inner
        - jnp.mean(inner, axis=-1, keepdims=True)
        - unit * jnp.mean(inner * unit, axis=-1, keepdims=True)
    )
    return (lower, jnp.sum(upper * unit, axis=0), jnp.sum(upper, axis=0))


def time_features(timesteps, width):
    half = width // 2
    frequency = jnp.exp(-math.log(10000.0) * jnp.arange(half, dtype=jnp.float32) / half)
    angles = timesteps.astype(jnp.float32)[:, None] * frequency[None, :]
    return jnp.concatenate([jnp.cos(angles), jnp.sin(angles)], axis=1)


def split_heads(value):
    return value.reshape(-1, L, value.shape[1] // HEAD_DIM, HEAD_DIM)


def project(start_rows, qkv_weight, qv_bias):
    total = start_rows.shape[0]
    joined = direct(start_rows, qkv_weight.reshape(qkv_weight.shape[0], -1), normal_dims).reshape(
        total, 3, -1
    )
    biases = qv_bias.astype(jnp.float32)
    query = (joined[:, 0] + biases[0]).astype(jnp.bfloat16)
    keys = joined[:, 1].astype(jnp.bfloat16)
    values = (joined[:, 2] + biases[1]).astype(jnp.bfloat16)
    return (query, keys, values)


def raw_scores(query, keys, lengths):
    scores = jnp.einsum(
        "sqhd,skhd->shqk", split_heads(query), split_heads(keys), preferred_element_type=jnp.float32
    ) * HEAD_DIM ** (-0.5)
    valid = jnp.arange(L, dtype=jnp.int32)[None, :] < lengths[:, None]
    return jnp.where(valid[:, None, None, :], scores, -1e30)


def mix(probs, values):
    heads = jnp.einsum(
        "shqk,skhd->sqhd",
        probs.astype(jnp.bfloat16),
        split_heads(values),
        preferred_element_type=jnp.float32,
    )
    return heads.reshape(-1, heads.shape[2] * heads.shape[3]).astype(jnp.bfloat16)


def attn_forward(start_rows, qkv_weight, qv_bias, out_weight, lengths):
    query, keys, values = project(start_rows, qkv_weight, qv_bias)
    scores = raw_scores(query, keys, lengths)
    top = jnp.max(scores, axis=-1, keepdims=True)
    expo = jnp.exp(scores - top)
    total_exp = jnp.sum(expo, axis=-1, keepdims=True)
    logsum = top + jnp.log(total_exp)
    mixed = mix(expo / total_exp, values)
    return (direct(mixed, out_weight, normal_dims), logsum)


def attn_backward(start_rows, grad_attn, qkv_weight, qv_bias, out_weight, lengths, logsum):
    query, keys, values = project(start_rows, qkv_weight, qv_bias)
    probs = jnp.exp(raw_scores(query, keys, lengths) - logsum)
    probs_low = probs.astype(jnp.bfloat16)
    mixed_again = mix(probs, values)
    grad_wout = direct(mixed_again, grad_attn, trans_left)
    grad_heads = split_heads(direct(grad_attn, out_weight, trans_right).astype(jnp.bfloat16))
    grad_values = jnp.einsum(
        "shqk,sqhd->skhd", probs_low, grad_heads, preferred_element_type=jnp.float32
    )
    grad_probs = jnp.einsum(
        "sqhd,skhd->shqk", grad_heads, split_heads(values), preferred_element_type=jnp.float32
    )
    delta = jnp.sum(grad_probs * probs, axis=-1, keepdims=True)
    grad_scores = (probs * (grad_probs - delta)).astype(jnp.bfloat16)
    scale = HEAD_DIM ** (-0.5)
    grad_query = (
        jnp.einsum(
            "shqk,skhd->sqhd", grad_scores, split_heads(keys), preferred_element_type=jnp.float32
        )
        * scale
    )
    grad_keys = (
        jnp.einsum(
            "shqk,sqhd->skhd", grad_scores, split_heads(query), preferred_element_type=jnp.float32
        )
        * scale
    )
    total = start_rows.shape[0]
    grad_joined = jnp.stack(
        [
            grad_query.reshape(total, -1),
            grad_keys.reshape(total, -1),
            grad_values.reshape(total, -1),
        ],
        axis=1,
    ).astype(jnp.bfloat16)
    grad_flat = grad_joined.reshape(total, -1)
    grad_qkv = direct(start_rows, grad_flat, trans_left).reshape(qkv_weight.shape)
    grad_sums = jnp.sum(grad_joined.astype(jnp.float32), axis=0)
    grad_qvbias = jnp.stack([grad_sums[0], grad_sums[2]], axis=0)
    grad_input = direct(grad_flat, qkv_weight.reshape(qkv_weight.shape[0], -1), trans_right)
    return (grad_qkv, grad_qvbias, grad_wout, grad_input)


def local(
    tokens,
    timesteps,
    lengths,
    time_inner,
    time_ibias,
    time_outer,
    time_obias,
    qkv_weight,
    qv_bias,
    out_weight,
    out_bias,
    gain_first,
    shift_first,
    up_weight,
    up_bias,
    down_weight,
    down_bias,
    gain_second,
    shift_second,
    cotangent,
):
    rows, width = tokens.shape
    features = time_features(timesteps, time_inner.shape[0])
    touter = time_outer.astype(jnp.float32)
    inner_pre = exact(features, time_inner.astype(jnp.float32), normal_dims) + time_ibias.astype(
        jnp.float32
    )
    inner_act, silu_back = jax.vjp(jax.nn.silu, inner_pre)
    temb = exact(inner_act, touter, normal_dims) + time_obias.astype(jnp.float32)
    start = (tokens.astype(jnp.float32).reshape(-1, L, width) + temb[:, None, :]).reshape(
        rows, width
    )
    start_low = start.astype(jnp.bfloat16)
    start_all = lax.all_gather(start_low, "tensor", axis=0, tiled=True)
    attn_terms, logsum = attn_forward(start_all, qkv_weight, qv_bias, out_weight, lengths)
    attn = lax.psum_scatter(attn_terms, "tensor", scatter_dimension=0, tiled=True)
    first = start + attn + out_bias.astype(jnp.float32)
    normed, unit_first, scaled_first = norm_forward(
        first, gain_first.astype(jnp.float32), shift_first.astype(jnp.float32)
    )
    normed_low = normed.astype(jnp.bfloat16)
    normed_all = lax.all_gather(normed_low, "tensor", axis=0, tiled=True)
    pre = direct(normed_all, up_weight, trans_right) + up_bias.astype(jnp.float32)
    act_low = gelu_exact(pre).astype(jnp.bfloat16)
    mlp = lax.psum_scatter(
        direct(act_low, down_weight, normal_dims), "tensor", scatter_dimension=0, tiled=True
    )
    second = normed + mlp + down_bias.astype(jnp.float32)
    result, unit_second, scaled_second = norm_forward(
        second, gain_second.astype(jnp.float32), shift_second.astype(jnp.float32)
    )
    layer_out = result.astype(jnp.bfloat16)
    grad_second, grad_gsecond, grad_ssecond = norm_backward(
        cotangent.astype(jnp.float32), unit_second, scaled_second, gain_second.astype(jnp.float32)
    )
    grad_bdown = jnp.sum(grad_second, axis=0)
    grad_low = grad_second.astype(jnp.bfloat16)
    grad_all, normed_again = (
        lax.all_gather(grad_low, "tensor", axis=0, tiled=True),
        lax.all_gather(normed_low, "tensor", axis=0, tiled=True),
    )
    pre_again = direct(normed_again, up_weight, trans_right) + up_bias.astype(jnp.float32)
    act_again, gelu_again = jax.vjp(gelu_exact, pre_again)
    grad_wdown = direct(act_again.astype(jnp.bfloat16), grad_all, trans_left)
    grad_act = direct(grad_all, down_weight, trans_right)
    grad_pre = gelu_again(grad_act)[0].astype(jnp.bfloat16)
    grad_wup = direct(grad_pre, normed_again, trans_left)
    grad_bup = jnp.sum(grad_pre.astype(jnp.float32), axis=0)
    grad_normed = grad_second + lax.psum_scatter(
        direct(grad_pre, up_weight, normal_dims), "tensor", scatter_dimension=0, tiled=True
    )
    grad_first, grad_gfirst, grad_sfirst = norm_backward(
        grad_normed, unit_first, scaled_first, gain_first.astype(jnp.float32)
    )
    grad_bout = jnp.sum(grad_first, axis=0)
    attn_grad_low = grad_first.astype(jnp.bfloat16)
    grad_attn, start_again = (
        lax.all_gather(attn_grad_low, "tensor", axis=0, tiled=True),
        lax.all_gather(start_low, "tensor", axis=0, tiled=True),
    )
    grad_qkv, grad_qvbias, grad_wout, grad_input = attn_backward(
        start_again, grad_attn, qkv_weight, qv_bias, out_weight, lengths, logsum
    )
    grad_tokens = grad_first + lax.psum_scatter(
        grad_input.astype(jnp.bfloat16), "tensor", scatter_dimension=0, tiled=True
    ).astype(jnp.float32)
    grad_temb = jnp.sum(grad_tokens.reshape(-1, L, width), axis=1)
    grad_touter = exact(inner_act, grad_temb, trans_left)
    grad_tobias = jnp.sum(grad_temb, axis=0)
    grad_hidden = silu_back(exact(grad_temb, touter, trans_right))[0]
    grad_tinner = exact(features, grad_hidden, trans_left)
    grad_tibias = jnp.sum(grad_hidden, axis=0)
    grad_qkv, grad_qvbias, grad_wout, grad_wup, grad_bup, grad_wdown = lax.psum(
        (grad_qkv, grad_qvbias, grad_wout, grad_wup, grad_bup, grad_wdown), "dp"
    )
    (
        grad_tinner,
        grad_tibias,
        grad_touter,
        grad_tobias,
        grad_bout,
        grad_gfirst,
        grad_sfirst,
        grad_bdown,
        grad_gsecond,
        grad_ssecond,
    ) = lax.psum(
        (
            grad_tinner,
            grad_tibias,
            grad_touter,
            grad_tobias,
            grad_bout,
            grad_gfirst,
            grad_sfirst,
            grad_bdown,
            grad_gsecond,
            grad_ssecond,
        ),
        ("dp", "tensor"),
    )
    return (
        layer_out,
        grad_tokens,
        grad_tinner,
        grad_tibias,
        grad_touter,
        grad_tobias,
        grad_qkv,
        grad_qvbias,
        grad_wout,
        grad_bout,
        grad_gfirst,
        grad_sfirst,
        grad_wup,
        grad_bup,
        grad_wdown,
        grad_bdown,
        grad_gsecond,
        grad_ssecond,
    )


def solution(mesh):
    placed = (
        P(("dp", "tensor"), None),
        P(("dp", "tensor")),
        P("dp"),
        P(),
        P(),
        P(),
        P(),
        P(None, None, "tensor"),
        P(None, "tensor"),
        P("tensor", None),
        P(),
        P(),
        P(),
        P("tensor", None),
        P("tensor"),
        P("tensor", None),
        P(),
        P(),
        P(),
        P(("dp", "tensor"), None),
    )
    return jax.shard_map(
        local,
        mesh=mesh,
        in_specs=placed,
        out_specs=(
            P(("dp", "tensor"), None),
            P(("dp", "tensor"), None),
            P(),
            P(),
            P(),
            P(),
            P(None, None, "tensor"),
            P(None, "tensor"),
            P("tensor", None),
            P(),
            P(),
            P(),
            P("tensor", None),
            P("tensor"),
            P("tensor", None),
            P(),
            P(),
            P(),
        ),
        check_vma=False,
    )
```

profile of v0, /device:TPU:0, one launch (start us, length us, event | category | flops | bytes accessed | tf_op | source)
XLA Modules:
  0.0 994.8 jit_solution(14979197148704922850)
XLA Ops:
  14.1 2.5 fusion.22
  16.9 40.0 %all-gather.5.cloned.1.call-done = bf16[3072,768]{1,0:T(8,128)(2,1)} async-done(((bf16[768,768]{1,0:T(8,128)(2,1)}), bf16[3072,768]{1,0:T(8,128)(2,1)}) %all-gather.5.cloned.1.call-update) | async-done | bytes 4718608 | tf_op jit(solution)/shard_map/all_gather | solution.py:185
  56.9 4.8 fusion.8
  64.7 1.7 fusion.67
  70.6 5.1 fusion.33
  76.4 77.9 %reduce-scatter.5.cloned.1.call-done = f32[768,768]{1,0:T(8,128)} async-done(((f32[3072,768]{1,0:T(8,128)}), f32[768,768]{1,0:T(8,128)}) %reduce-scatter.5.cloned.1.call-update) | async-done | bytes 2359312 | tf_op jit(solution)/shard_map/reduce_scatter | solution.py:187
  154.3 2.5 fusion.65
  160.2 36.1 %all-gather.7.cloned.1.call-done = bf16[3072,768]{1,0:T(8,128)(2,1)} async-done(((bf16[768,768]{1,0:T(8,128)(2,1)}), bf16[3072,768]{1,0:T(8,128)(2,1)}) %all-gather.7.cloned.1.call-update) | async-done | bytes 4718608 | tf_op jit(solution)/shard_map/all_gather | solution.py:193
  196.3 26.3 %multiply_convert_fusion = (bf16[3072,768]{1,0:T(8,128)(2,1)S(1)}, f32[3072,768]{1,0:T(8,128)}, f32[3072,768]{1,0:T(8,128)}) fusion(f32[768]{0:T(1024)} %convert_element_type.150, bf16[3072,768]{1,0:T(8,128)(2,1)} %all-gather.7.cloned.1.call-done, bf16[768,768]{1,0:T(8,128)(2,1)S(1)} %copy-done), kind=kOutput, calls=%fused_computation.5 | convolution fusion | flops 3779592192 | bytes 29494272 | tf_op jit(solution)/shard_map/dot_general | solution.py:29
  222.7 2.2 copy-done.56
  224.9 6.2 fusion.68
  235.0 74.6 %reduce-scatter.7.cloned.1.call-done = f32[768,768]{1,0:T(8,128)} async-done(((f32[3072,768]{1,0:T(8,128)}), f32[768,768]{1,0:T(8,128)}) %reduce-scatter.7.cloned.1.call-update) | async-done | bytes 2359312 | tf_op jit(solution)/shard_map/reduce_scatter | solution.py:196
  309.6 2.5 fusion.63
  315.1 2.5 fusion.57
  320.6 37.2 %all-gather.9.cloned.1.call-done = bf16[3072,768]{1,0:T(8,128)(2,1)} async-done(((bf16[768,768]{1,0:T(8,128)(2,1)}), bf16[3072,768]{1,0:T(8,128)(2,1)}) %all-gather.9.cloned.1.call-update) | async-done | bytes 4718608 | tf_op jit(solution)/shard_map/all_gather | solution.py:210
  357.8 13.5 %convert_reduce_fusion = (f32[768]{0:T(1024)}, bf16[3072,768]{1,0:T(8,128)(2,1)S(1)}) fusion(f32[3072,768]{1,0:T(8,128)} %get-tuple-element.60, f32[3072,768]{1,0:T(8,128)} %get-tuple-element.72, f32[768]{0:T(1024)S(1)} %copy-done.47, bf16[3072,768]{1,0:T(8,128)(2,1)} %all-gather.9.cloned.1.call-done, bf16[768,768]{1,0:T(8,128)(2,1)} %param.35), kind=kOutput, calls=%fused_computation.3 | convolution fusion | flops 3663985920 | bytes 29497344 | tf_op jit(solution)/shard_map/dot_general | solution.py:29
  371.3 2.2 copy-done.57
  373.5 6.4 fusion.69
  380.0 78.5 %reduce-scatter.9.cloned.1.call-done = f32[768,768]{1,0:T(8,128)} async-done(((f32[3072,768]{1,0:T(8,128)}), f32[768,768]{1,0:T(8,128)}) %reduce-scatter.9.cloned.1.call-update) | async-done | bytes 2359312 | tf_op jit(solution)/shard_map/reduce_scatter | solution.py:220
  458.5 4.2 multiply_reduce_fusion.1
  467.0 37.3 %all-gather.11.cloned.1.call-done = bf16[3072,768]{1,0:T(8,128)(2,1)} async-done(((bf16[768,768]{1,0:T(8,128)(2,1)}), bf16[3072,768]{1,0:T(8,128)(2,1)}) %all-gather.11.cloned.1.call-update) | async-done | bytes 4718608 | tf_op jit(solution)/shard_map/all_gather | solution.py:229
  504.4 4.0 fusion.28
  509.7 4.0 multiply_reduce_fusion
  516.7 2.7 multiply_bitcast_fusion
  519.5 1.7 convolution_bitcast_fusion
  521.2 1.8 copy.57
  523.0 3.0 stack_reshape.9
  526.0 3.0 copy.59
  529.0 3.0 stack_reshape.10
  532.0 1.8 copy.62
  533.8 3.1 stack_reshape.11
  536.9 2.6 convert_reduce_fusion.1
  539.5 1.7 copy-done.13
  541.2 5.6 bitcast_convert_fusion
  547.6 3.2 fusion.26
  551.7 11.4 %fusion.71 = f32[768,768]{1,0:T(8,128)} fusion(bf16[3072,768]{1,0:T(8,128)(2,1)} %copy-done.56, bf16[3072,768]{1,0:T(8,128)(2,1)} %all-gather.9.cloned.1.call-done), kind=kOutput, calls=%fused_computation.131 | convolution fusion | flops 3623878656 | bytes 11796480 | tf_op jit(solution)/shard_map/dot_general | solution.py:29
  563.2 5.4 fusion.70
  568.6 1.9 fusion.30
  570.6 4.4 fusion.6
  575.0 19.8 %reduce-scatter.11.cloned.1.call-done = bf16[768,768]{1,0:T(8,128)(2,1)} async-done(((bf16[3072,768]{1,0:T(8,128)(2,1)}), bf16[768,768]{1,0:T(8,128)(2,1)}) %reduce-scatter.11.cloned.1.call-update) | async-done | bytes 1179664 | tf_op jit(solution)/shard_map/reduce_scatter | solution.py:235
  594.8 2.9 fusion.60
  597.8 1.9 reduce_sum.199
  601.7 2.6 fusion.49
  604.4 23.2 %all-reduce.2 = (f32[2,192]{1,0:T(2,128)}, f32[768]{0:T(1024)}) all-reduce(f32[2,192]{1,0:T(2,128)S(1)} %pad_maximum_fusion.1, f32[768]{0:T(1024)S(1)} %copy-done.46), channel_id=1, replica_groups=mesh['dp'=8,'tensor'=4] {'dp'}, use_global_device_ids=true, to_apply=%region_24.25 | all-reduce | flops 1152 | bytes 9216 | tf_op jit(solution)/shard_map/psum | solution.py:244
  627.6 40.7 %all-reduce = (f32[512]{0:T(512)}, f32[768]{0:T(1024)}, f32[768]{0:T(1024)}, f32[768]{0:T(1024)}, f32[768]{0:T(1024)}, /*index=5*/f32[768]{0:T(1024)}, f32[768]{0:T(1024)}, f32[768]{0:T(1024)}) all-reduce(f32[512]{0:T(512)S(1)} %get-tuple-element.54, ...), channel_id=1, replica_groups=mesh['dp'=8,'tensor'=4] {'dp','tensor'}, use_global_device_ids=true, to_apply=%region_18.19 | all-reduce | flops 5888 | bytes 47104 | tf_op jit(solution)/shard_map/psum | solution.py:258
  668.3 170.1 %all-reduce.9.cloned.1.call-done = (f32[768,3,192]{0,2,1:T(8,128)}, f32[192,768]{1,0:T(8,128)}, f32[768,768]{1,0:T(8,128)}, f32[768,768]{1,0:T(8,128)}) async-done(((f32[768,3,192]{0,2,1:T(8,128)}, f32[192,768]{1,0:T(8,128)}, f32[768,768]{1,0:T(8,128)}, f32[768,768]{1,0:T(8,128)}), (f32[768,3,192]{0,2,1:T(8,128)}, f32[192,768]{1,0:T(8,128)}, f32[768,768]{1,0:T(8,128)}, ...) | async-done | bytes 7077904 | tf_op jit(solution)/shard_map/psum | solution.py:244
  838.4 138.2 %all-reduce.7.cloned.1.call-done = (f32[128,512]{1,0:T(8,128)}, f32[512,768]{1,0:T(8,128)}) async-done(((f32[128,512]{1,0:T(8,128)}, f32[512,768]{1,0:T(8,128)}), (f32[128,512]{1,0:T(8,128)}, f32[512,768]{1,0:T(8,128)})) %all-reduce.7.cloned.1.call-update) | async-done | bytes 1835024 | tf_op jit(solution)/shard_map/psum | solution.py:258
  978.2 2.7 copy.113
  (214 shorter events, 48.7 us)
Async XLA Ops:
  7.2 189.1 %copy-start = (bf16[768,768]{1,0:T(8,128)(2,1)S(1)}, bf16[768,768]{1,0:T(8,128)(2,1)}, u32[]{:S(2)}) copy-start(bf16[768,768]{1,0:T(8,128)(2,1)} %param.33) | copy-start | bytes 3538948
  7.2 9.4 copy-start.51
  7.2 9.6 copy-start.52
  7.2 49.7 %copy-start.54 = (bf16[768,3,192]{0,2,1:T(8,128)(2,1)S(1)}, bf16[768,3,192]{0,2,1:T(8,128)(2,1)}, u32[]{:S(2)}) copy-start(bf16[768,3,192]{0,2,1:T(8,128)(2,1)} %param.27) | copy-start | bytes 2654212
  7.2 49.7 %all-gather.5.cloned.1.call-start = ((), (), s32[]{:S(2)}) async-start(), calls=%async_computation.4 | async-start | bytes 5898240 | tf_op jit(solution)/shard_map/all_gather | solution.py:185
  16.6 137.7 %reduce-scatter.5.cloned.1.call-start = ((), (), s32[]{:S(2)}) async-start(), calls=%async_computation.5 | async-start | bytes 11796480 | tf_op jit(solution)/shard_map/reduce_scatter | solution.py:187
  16.8 46.8 %copy-start.37 = (f32[3,64]{1,0:T(4,128)}, f32[3,64]{1,0:T(4,128)S(1)}, u32[]{:S(2)}) copy-start(f32[3,64]{1,0:T(4,128)S(1)} %add.192) | copy-start | bytes 2308
  75.7 120.6 %all-gather.7.cloned.1.call-start = ((), (), s32[]{:S(2)}) async-start(), calls=%async_computation.6 | async-start | bytes 5898240 | tf_op jit(solution)/shard_map/all_gather | solution.py:193
  158.7 150.9 %reduce-scatter.7.cloned.1.call-start = ((), (), s32[]{:S(2)}) async-start(), calls=%async_computation.7 | async-start | bytes 11796480 | tf_op jit(solution)/shard_map/reduce_scatter | solution.py:196
  196.3 28.6 %copy-start.53 = (bf16[768,768]{1,0:T(8,128)(2,1)S(1)}, bf16[768,768]{1,0:T(8,128)(2,1)}, u32[]{:S(2)}) copy-start(bf16[768,768]{1,0:T(8,128)(2,1)} %param.35) | copy-start | bytes 3538948
  222.7 2.2 copy-start.56
  231.1 126.6 %all-gather.9.cloned.1.call-start = ((), (), s32[]{:S(2)}) async-start(), calls=%async_computation.8 | async-start | bytes 5898240 | tf_op jit(solution)/shard_map/all_gather | solution.py:210
  312.6 2.5 copy-start.42
  319.0 38.8 %copy-start.47 = (f32[768]{0:T(1024)S(1)}, f32[768]{0:T(1024)}, u32[]{:S(2)}) copy-start(f32[768]{0:T(1024)} %convert_element_type.150) | copy-start | bytes 9220
  320.1 138.3 %reduce-scatter.9.cloned.1.call-start = ((), (), s32[]{:S(2)}) async-start(), calls=%async_computation.9 | async-start | bytes 11796480 | tf_op jit(solution)/shard_map/reduce_scatter | solution.py:220
  371.3 2.2 copy-start.57
  379.9 124.4 %all-gather.11.cloned.1.call-start = ((), (), s32[]{:S(2)}) async-start(), calls=%async_computation.10 | async-start | bytes 5898240 | tf_op jit(solution)/shard_map/all_gather | solution.py:229
  465.6 38.8 %copy-start.26 = (bf16[192,768]{1,0:T(8,128)(2,1)S(1)}, bf16[192,768]{1,0:T(8,128)(2,1)}, u32[]{:S(2)}) copy-start(bf16[192,768]{1,0:T(8,128)(2,1)} %param.29) | copy-start | bytes 884740
  466.7 128.1 %reduce-scatter.11.cloned.1.call-start = ((), (), s32[]{:S(2)}) async-start(), calls=%async_computation.11 | async-start | bytes 5898240 | tf_op jit(solution)/shard_map/reduce_scatter | solution.py:235
  467.0 46.6 %copy-start.19 = (f32[24,3,128]{2,1,0:T(4,128)}, f32[24,3,128]{2,1,0:T(4,128)S(1)}, u32[]{:S(2)}) copy-start(f32[24,3,128]{2,1,0:T(4,128)S(1)} %log_add_fusion) | copy-start | bytes 110596
  508.6 5.1 slice-start
  509.7 4.0 slice-start.1
  516.7 2.7 copy-start.20
  533.8 3.1 copy-start.11
  536.9 4.4 copy-start.55
  546.8 291.5 %all-reduce.9.cloned.1.call-start = ((), (), s32[]{:S(2)}) async-start(), calls=%async_computation.13 | async-start | bytes 14155776 | tf_op jit(solution)/shard_map/psum | solution.py:244
  547.6 15.5 %slice-start.4 = ((s8[4718592]{0:T(1024)(128)(4,1)}), s8[4194304]{0:T(1024)(128)(4,1)S(1)}, s32[]{:S(2)}) async-start(s8[4718592]{0:T(1024)(128)(4,1)} %bitcast.135), calls=%async_computation.18 | async-start | bytes 8388608
  550.9 12.3 %slice-start.8 = ((s8[4718592]{0:T(1024)(128)(4,1)}), s8[4194304]{0:T(1024)(128)(4,1)S(1)}, s32[]{:S(2)}) async-start(s8[4718592]{0:T(1024)(128)(4,1)} %bitcast.139), calls=%async_computation.22 | async-start | bytes 8388608
  551.6 11.5 %slice-start.5 = ((s8[4718592]{0:T(1024)(128)(4,1)}), s8[524288]{0:T(1024)(128)(4,1)S(1)}, s32[]{:S(2)}) async-start(s8[4718592]{0:T(1024)(128)(4,1)} %bitcast.135), calls=%async_computation.19 | async-start | bytes 1048576
  551.7 11.5 %slice-start.9 = ((s8[4718592]{0:T(1024)(128)(4,1)}), s8[524288]{0:T(1024)(128)(4,1)S(1)}, s32[]{:S(2)}) async-start(s8[4718592]{0:T(1024)(128)(4,1)} %bitcast.139), calls=%async_computation.23 | async-start | bytes 1048576
  551.7 16.9 %slice-start.6 = ((s8[4718592]{0:T(1024)(128)(4,1)}), s8[4194304]{0:T(1024)(128)(4,1)S(1)}, s32[]{:S(2)}) async-start(s8[4718592]{0:T(1024)(128)(4,1)} %bitcast.137), calls=%async_computation.20 | async-start | bytes 8388608
  551.7 18.8 %slice-start.2 = ((s8[4718592]{0:T(1024)(128)(4,1)}), s8[4194304]{0:T(1024)(128)(4,1)S(1)}, s32[]{:S(2)}) async-start(s8[4718592]{0:T(1024)(128)(4,1)} %bitcast.133), calls=%async_computation.16 | async-start | bytes 8388608
  563.2 5.4 slice-start.7
  563.2 7.3 slice-start.3
  574.9 19.9 %copy-start.6 = (f32[768,768]{1,0:T(8,128)S(1)}, f32[768,768]{1,0:T(8,128)}, u32[]{:S(2)}) copy-start(f32[768,768]{1,0:T(8,128)} %copy-done.5) | copy-start | bytes 7077892
  575.0 401.6 %all-reduce.7.cloned.1.call-start = ((), (), s32[]{:S(2)}) async-start(), calls=%async_computation.12 | async-start | bytes 3670016 | tf_op jit(solution)/shard_map/psum | solution.py:258
  597.8 2.7 copy-start.33
  597.8 2.8 copy-start.35
  599.7 4.7 copy-start.45
  599.7 4.7 copy-start.46
  599.7 27.9 %copy-start.39 = (f32[768]{0:T(1024)S(1)}, f32[768]{0:T(1024)}, u32[]{:S(2)}) copy-start(f32[768]{0:T(1024)} %get-tuple-element.23) | copy-start | bytes 9220
  599.7 27.9 %copy-start.40 = (f32[768]{0:T(1024)S(1)}, f32[768]{0:T(1024)}, u32[]{:S(2)}) copy-start(f32[768]{0:T(1024)} %get-tuple-element.48) | copy-start | bytes 9220
  599.7 27.9 %copy-start.41 = (f32[768]{0:T(1024)S(1)}, f32[768]{0:T(1024)}, u32[]{:S(2)}) copy-start(f32[768]{0:T(1024)} %get-tuple-element.50) | copy-start | bytes 9220
  599.7 27.8 %copy-start.43 = (f32[768]{0:T(1024)S(1)}, f32[768]{0:T(1024)}, u32[]{:S(2)}) copy-start(f32[768]{0:T(1024)} %get-tuple-element.20) | copy-start | bytes 9220
  599.8 27.8 %copy-start.44 = (f32[768]{0:T(1024)S(1)}, f32[768]{0:T(1024)}, u32[]{:S(2)}) copy-start(f32[768]{0:T(1024)} %get-tuple-element.25) | copy-start | bytes 9220
  838.4 142.5 %copy-start.18 = (f32[768,3,192]{0,2,1:T(8,128)S(1)}, f32[768,3,192]{0,2,1:T(8,128)}, u32[]{:S(2)}) copy-start(f32[768,3,192]{0,2,1:T(8,128)} %get-tuple-element.83) | copy-start | bytes 5308420
  980.9 2.7 copy-start.17
  983.6 2.5 copy-start.16
  (30 other events, 40.9 us)
Sparse Core Ops, SparseCore 0:
  16.7 40.1 all-gather.4
  75.9 78.4 reduce-scatter.4
  158.8 37.4 all-gather.6
  231.2 78.3 reduce-scatter.6
  320.3 37.4 all-gather.8
  380.0 78.4 reduce-scatter.8
  466.9 37.4 all-gather.10
  547.0 47.8 reduce-scatter.10
  601.0 237.2 all-reduce.8
  844.4 132.1 all-reduce.6
where the time goes:
time: 1000 us; the launch traced here: 995 us
  waiting for transfers between devices  710 us (71%)
  matrix products  117 us (12%)
  blocking collectives  63.9 us (6%)
  local copies, waits for them, and re-layouts  47.2 us (5%)
  other arithmetic  39.8 us (4%)
  between operations  15.3 us (2%)
    psum x1, waiting for transfers between devices, local(): lax.psum((grad_qkv, grad_qvbias, grad_wout, grad_wup, grad_bup, grad_wdow...  170 us
    psum x1, waiting for transfers between devices, local(): lax.psum((grad_tinner, grad_tibias, grad_touter, grad_tobias, grad_bout,...  138 us
    dot_general x12, matrix products, direct(): lax.dot_general(left, right, (dims, ((), ())), preferred_element_type=jnp...  95 us
    reduce_scatter x1, waiting for transfers between devices, local(): lax.psum_scatter(direct(grad_pre, up_weight, normal_dims), 'tensor', scat...  78.5 us
    reduce_scatter x1, waiting for transfers between devices, local(): lax.psum_scatter(attn_terms, 'tensor', scatter_dimension=0, tiled=True)  77.9 us
    reduce_scatter x1, waiting for transfers between devices, local(): lax.psum_scatter(direct(act_low, down_weight, normal_dims), 'tensor', sca...  74.6 us
    psum x1, blocking collectives, local(): lax.psum((grad_tinner, grad_tibias, grad_touter, grad_tobias, grad_bout,...  40.7 us
    all_gather x1, waiting for transfers between devices, local(): start_all = lax.all_gather(start_low, 'tensor', axis=0, tiled=True)  40 us
  transfers between devices with their start and end apart: 10, of which 10 were waited for; matrix products, arithmetic and copies ran while one was open for 4% of the time, Pallas kernels for 0%

commit v1 on v0

v1 whole, which is shorter than its diff:
```python
import functools
import math

import jax
import jax.numpy as jnp
from jax import lax
from jax.experimental import pallas as pl
from jax.experimental.pallas import tpu as pltpu
from jax.sharding import PartitionSpec as P

L = 128
HD = 64
EPS = 1e-05
F32 = jnp.float32
BF = jnp.bfloat16
NN = ((1,), (0,))
NT = ((1,), (1,))
TN = ((0,), (0,))
VMEM_LIMIT = 56 * 1024 * 1024


def dot(left, right, dims):
    return lax.dot_general(left, right, (dims, ((), ())), preferred_element_type=F32)


def exact(left, right, dims):
    return lax.dot_general(
        left, right, (dims, ((), ())), precision=lax.Precision.HIGHEST, preferred_element_type=F32
    )


def call(body, outs, args, flops, scratch=(), smem=()):
    moved = sum(math.prod(o.shape) * o.dtype.itemsize for o in outs)
    moved += sum(math.prod(a.shape) * a.dtype.itemsize for a in args)
    return pl.pallas_call(
        body,
        out_shape=outs,
        in_specs=[
            pl.BlockSpec(memory_space=pltpu.SMEM if i in smem else pltpu.VMEM)
            for i in range(len(args))
        ],
        out_specs=[pl.BlockSpec(memory_space=pltpu.VMEM) for _ in outs],
        scratch_shapes=list(scratch),
        cost_estimate=pl.CostEstimate(flops=int(flops), bytes_accessed=int(moved), transcendentals=0),
        compiler_params=pltpu.CompilerParams(vmem_limit_bytes=VMEM_LIMIT),
    )(*args)


def sds(shape, dtype):
    return jax.ShapeDtypeStruct(shape, dtype)


def pieces(a, b, lo, hi):
    return [a[lo:hi, :], b[lo:hi, :]]


def head_mask(width):
    lane = lax.broadcasted_iota(jnp.int32, (1, width), 1)
    first = jnp.where(lane < width // 2, 1.0, 0.0)
    return first.astype(BF), (1.0 - first).astype(BF)


def doubled(pair, masks):
    return jnp.concatenate([pair * masks[0], pair * masks[1]], axis=0)


def joined_weight(a_ref, b_ref, w):
    parts = []
    for k in range(3):
        parts += pieces(a_ref, b_ref, k * w, (k + 1) * w)
    return jnp.concatenate(parts, axis=0)


def attn_fwd_core(x, a_ref, b_ref, len_ref, qkv_ref, p_ref, mix_ref):
    w = a_ref.shape[1] // 4
    rows = x.shape[0]
    seqs = rows // L
    wide = 2 * w
    big = joined_weight(a_ref, b_ref, w)
    base = 4 * w
    qb = (a_ref[base : base + 1, :] + b_ref[base + 1 : base + 2, :]).astype(F32)
    vb = (a_ref[base + 2 : base + 3, :] + b_ref[base + 3 : base + 4, :]).astype(F32)
    total = dot(x, big, NT)
    qkv_ref[:, :wide] = (total[:, :wide] + qb[:, :wide]).astype(BF)
    qkv_ref[:, wide : 2 * wide] = total[:, wide : 2 * wide].astype(BF)
    qkv_ref[:, 2 * wide :] = (total[:, 2 * wide :] + vb[:, :wide]).astype(BF)
    masks = head_mask(2 * HD)
    key_at = lax.broadcasted_iota(jnp.int32, (L, L), 0)
    pairs = wide // (2 * HD)

    def one(s, carry):
        at = pl.ds(pl.multiple_of(s * L, L), L)
        valid = key_at < len_ref[s]
        for pair in range(pairs):
            lo = pair * 2 * HD
            q = qkv_ref[at, lo : lo + 2 * HD]
            k = qkv_ref[at, wide + lo : wide + lo + 2 * HD]
            v = qkv_ref[at, 2 * wide + lo : 2 * wide + lo + 2 * HD]
            scores = dot(doubled(k, masks), q, NT) * HD ** (-0.5)
            lows = []
            for h in range(2):
                part = jnp.where(valid, scores[h * L : (h + 1) * L], -1e30)
                expo = jnp.exp(part - jnp.max(part, axis=0, keepdims=True))
                prob = expo * (1.0 / jnp.sum(expo, axis=0, keepdims=True))
                p_ref[s * pairs + pair, h * L : (h + 1) * L, :] = prob
                lows.append(prob.astype(BF))
            mixed = dot(jnp.concatenate(lows, axis=0), doubled(v, masks), TN)
            mix_ref[at, lo : lo + 2 * HD] = mixed.astype(BF)
        return carry

    lax.fori_loop(0, seqs, one, 0)
    out = jnp.concatenate(pieces(a_ref, b_ref, 3 * w, 4 * w), axis=0)
    return dot(mix_ref[...], out, NN)


def start_of(tok_ref, temb_ref):
    rows, width = tok_ref.shape
    seqs = rows // L
    return [
        tok_ref[s * L : (s + 1) * L, :].astype(F32) + temb_ref[s : s + 1, :] for s in range(seqs)
    ]


def attn_near_body(len_ref, tok_ref, temb_ref, a_ref, b_ref, x_ref, qkv_ref, p_ref, mix_ref, acc_ref):
    for s, rows in enumerate(start_of(tok_ref, temb_ref)):
        x_ref[s * L : (s + 1) * L, :] = rows.astype(BF)
    acc_ref[...] = attn_fwd_core(x_ref[...], a_ref, b_ref, len_ref, qkv_ref, p_ref, mix_ref)


def row_mean(value):
    return jnp.mean(value, axis=-1, keepdims=True)


def unit_of(value):
    centred = value - row_mean(value)
    rate = lax.rsqrt(row_mean(centred * centred) + EPS)
    return centred * rate, rate


def attn_far_body(
    len_ref, tok_ref, temb_ref, x_ref, a_ref, b_ref, near_ref, vec_ref,
    qkv_ref, p_ref, mix_ref, first_ref, low_ref,
):
    acc = attn_fwd_core(x_ref[...], a_ref, b_ref, len_ref, qkv_ref, p_ref, mix_ref)
    first_ref[...] = acc + near_ref[...] + vec_ref[0:1, :]
    for s, rows in enumerate(start_of(tok_ref, temb_ref)):
        at = slice(s * L, (s + 1) * L)
        first = first_ref[at, :] + rows
        first_ref[at, :] = first
        unit, _ = unit_of(first)
        low_ref[at, :] = (unit * vec_ref[1:2, :] + vec_ref[2:3, :]).astype(BF)


def gelu_pair(pre):
    cdf = 0.5 * (1.0 + lax.erf(pre * 0.7071067811865476))
    pdf = jnp.exp(-0.5 * pre * pre) * 0.3989422804014327
    return pre * cdf, cdf + pre * pdf


def mlp_fwd_core(x_ref, ups, downs, biases, act_ref, slope_ref, acc_ref):
    rows = x_ref.shape[0]
    hid = ups[0].shape[0]
    tile = 384 if hid % 384 == 0 else hid
    block = 256 if rows % 256 == 0 else rows
    first = True
    for r in range(len(ups)):
        for t in range(hid // tile):
            up = ups[r][t * tile : (t + 1) * tile, :]
            down = downs[r][t * tile : (t + 1) * tile, :]
            bias = biases[r][:, t * tile : (t + 1) * tile].astype(F32)
            lo = r * hid + t * tile
            for m in range(rows // block):
                at = slice(m * block, (m + 1) * block)
                act, slope = gelu_pair(dot(x_ref[at, :], up, NT) + bias)
                low = act.astype(BF)
                act_ref[at, lo : lo + tile] = low
                slope_ref[at, lo : lo + tile] = slope
                part = dot(low, down, NN)
                if first:
                    acc_ref[at, :] = part
                else:
                    acc_ref[at, :] += part
            first = False


def mlp_near_body(x_ref, ua, ub, da, db, ba, bb, act_ref, slope_ref, acc_ref):
    row = 4
    mlp_fwd_core(
        x_ref, (ua, ub), (da, db), (ba[row : row + 1, :], bb[row : row + 1, :]),
        act_ref, slope_ref, acc_ref,
    )


def mlp_far_body(
    x_ref, ua, ub, da, db, ba, bb, near_ref, first_ref, vec_ref, cot_ref,
    act_ref, slope_ref, out_ref, grad_ref, sums_ref, acc_ref,
):
    row = 4
    mlp_fwd_core(
        x_ref, (ua, ub), (da, db), (ba[row : row + 1, :], bb[row : row + 1, :]),
        act_ref, slope_ref, acc_ref,
    )
    rows, width = x_ref.shape
    gain1, shift1, bias = vec_ref[1:2, :], vec_ref[2:3, :], vec_ref[3:4, :]
    gain, shift = vec_ref[4:5, :], vec_ref[5:6, :]
    sums_ref[...] = jnp.zeros_like(sums_ref)
    for s in range(rows // L):
        at = slice(s * L, (s + 1) * L)
        unit1, _ = unit_of(first_ref[at, :])
        normed = unit1 * gain1 + shift1
        second = normed + acc_ref[at, :] + near_ref[at, :] + bias
        unit, rate = unit_of(second)
        out_ref[at, :] = (unit * gain + shift).astype(BF)
        grad_out = cot_ref[at, :].astype(F32)
        inner = grad_out * gain
        lower = rate * (inner - row_mean(inner) - unit * row_mean(inner * unit))
        grad_ref[at, :] = lower
        sums_ref[0:1, :] += jnp.sum(grad_out * unit, axis=0, keepdims=True)
        sums_ref[1:2, :] += jnp.sum(grad_out, axis=0, keepdims=True)
        sums_ref[2:3, :] += jnp.sum(lower, axis=0, keepdims=True)


def mlp_bwd_core(x_ref, gl, ups, downs, act_ref, slope_ref, dus, dds, bsum_ref, acc_ref):
    hid = ups[0].shape[0]
    rows = x_ref.shape[0]
    for r in (1, 0):
        lo = r * hid
        dds[r][...] = dot(act_ref[:, lo : lo + hid], gl, TN).astype(dds[r].dtype)
        gp = (dot(gl, downs[r][...], NT) * slope_ref[:, lo : lo + hid]).astype(BF)
        bsum_ref[r : r + 1, :] = jnp.sum(gp.astype(F32), axis=0, keepdims=True)
        dus[r][...] = dot(gp, x_ref[...], TN).astype(dus[r].dtype)
        part = dot(gp, ups[r][...], NN)
        if r == 1:
            acc_ref[...] = part
        else:
            acc_ref[...] += part


def mlp_bwd_far_body(
    x_ref, g_ref, ua, ub, da, db, act_ref, slope_ref,
    dua, dub, dda, ddb, bsum_ref, acc_ref,
):
    bsum_ref[...] = jnp.zeros_like(bsum_ref)
    gl = g_ref[...].astype(BF)
    mlp_bwd_core(
        x_ref, gl, (ua, ub), (da, db), act_ref, slope_ref, (dua, dub), (dda, ddb), bsum_ref, acc_ref
    )


def mlp_bwd_near_body(
    x_ref, g_ref, ua, ub, da, db, act_ref, slope_ref, far_ref, first_ref, vec_ref,
    dua, dub, dda, ddb, bsum_ref, gf_ref, sums_ref,
):
    bsum_ref[...] = jnp.zeros_like(bsum_ref)
    gl = g_ref[...].astype(BF)
    mlp_bwd_core(
        x_ref, gl, (ua, ub), (da, db), act_ref, slope_ref, (dua, dub), (dda, ddb), bsum_ref, gf_ref
    )
    rows, width = x_ref.shape
    gain = vec_ref[1:2, :]
    sums_ref[...] = jnp.zeros_like(sums_ref)
    for s in range(rows // L):
        at = slice(s * L, (s + 1) * L)
        unit, rate = unit_of(first_ref[at, :])
        upper = gf_ref[at, :] + far_ref[at, :] + g_ref[at, :]
        inner = upper * gain
        lower = rate * (inner - row_mean(inner) - unit * row_mean(inner * unit))
        gf_ref[at, :] = lower
        sums_ref[0:1, :] += jnp.sum(upper * unit, axis=0, keepdims=True)
        sums_ref[1:2, :] += jnp.sum(upper, axis=0, keepdims=True)
        sums_ref[2:3, :] += jnp.sum(lower, axis=0, keepdims=True)


def attn_bwd_core(x_ref, gl, a_ref, b_ref, qkv_ref, p_ref, mix_ref, da_ref, db_ref, bsum_ref, gm_ref, dj_ref):
    rows = x_ref.shape[0]
    seqs = rows // L
    w = a_ref.shape[1] // 4
    wide = 2 * w
    out = jnp.concatenate(pieces(a_ref, b_ref, 3 * w, 4 * w), axis=0)
    gm_ref[...] = dot(gl, out, NT).astype(BF)
    dout = dot(mix_ref[...], gl, TN)
    da_ref[3 * w : 4 * w, :] = dout[:w].astype(da_ref.dtype)
    db_ref[3 * w : 4 * w, :] = dout[w:].astype(db_ref.dtype)
    masks = head_mask(2 * HD)
    half = lax.broadcasted_iota(jnp.int32, (L, 2 * HD), 1) < HD
    pairs = wide // (2 * HD)
    scale = HD ** (-0.5)

    def one(s, carry):
        at = pl.ds(pl.multiple_of(s * L, L), L)
        for pair in range(pairs):
            lo = pair * 2 * HD
            q = qkv_ref[at, lo : lo + 2 * HD]
            k = qkv_ref[at, wide + lo : wide + lo + 2 * HD]
            v = qkv_ref[at, 2 * wide + lo : 2 * wide + lo + 2 * HD]
            go = gm_ref[at, lo : lo + 2 * HD]
            prob = p_ref[s * pairs + pair]
            dv = dot(prob.astype(BF), go, NN)
            dp = dot(doubled(v, masks), go, NT)
            lows = []
            for h in range(2):
                ph = prob[h * L : (h + 1) * L]
                dh = dp[h * L : (h + 1) * L]
                delta = jnp.sum(ph * dh, axis=0, keepdims=True)
                lows.append((ph * (dh - delta)).astype(BF))
            ds = jnp.concatenate(lows, axis=0)
            dk = dot(ds, q, NN)
            dq = dot(ds, doubled(k, masks), TN) * scale
            dj_ref[at, lo : lo + 2 * HD] = dq.astype(BF)
            dj_ref[at, wide + lo : wide + lo + 2 * HD] = (
                jnp.where(half, dk[:L], dk[L:]) * scale
            ).astype(BF)
            dj_ref[at, 2 * wide + lo : 2 * wide + lo + 2 * HD] = jnp.where(
                half, dv[:L], dv[L:]
            ).astype(BF)
        return carry

    lax.fori_loop(0, seqs, one, 0)
    dj = dj_ref[...]
    grads = dot(dj, x_ref[...], TN)
    for k in range(3):
        lo = k * wide
        da_ref[k * w : (k + 1) * w, :] = grads[lo : lo + w].astype(da_ref.dtype)
        db_ref[k * w : (k + 1) * w, :] = grads[lo + w : lo + wide].astype(db_ref.dtype)
    bsum_ref[...] = jnp.zeros_like(bsum_ref)
    bsum_ref[0:1, :] = jnp.sum(dj[:, :wide].astype(F32), axis=0, keepdims=True)
    bsum_ref[1:2, :] = jnp.sum(dj[:, 2 * wide :].astype(F32), axis=0, keepdims=True)
    return dot(dj, joined_weight(a_ref, b_ref, w), NN)


def attn_bwd_far_body(
    x_ref, g_ref, a_ref, b_ref, qkv_ref, p_ref, mix_ref,
    da_ref, db_ref, bsum_ref, acc_ref, gm_ref, dj_ref,
):
    gl = g_ref[...].astype(BF)
    acc_ref[...] = attn_bwd_core(
        x_ref, gl, a_ref, b_ref, qkv_ref, p_ref, mix_ref, da_ref, db_ref, bsum_ref, gm_ref, dj_ref
    )


def attn_bwd_near_body(
    x_ref, g_ref, a_ref, b_ref, qkv_ref, p_ref, mix_ref, far_ref,
    da_ref, db_ref, bsum_ref, gt_ref, temb_ref, gm_ref, dj_ref,
):
    gl = g_ref[...].astype(BF)
    gt_ref[...] = (
        attn_bwd_core(
            x_ref, gl, a_ref, b_ref, qkv_ref, p_ref, mix_ref, da_ref, db_ref, bsum_ref, gm_ref, dj_ref
        )
        + far_ref[...]
        + g_ref[...]
    )
    temb_ref[...] = jnp.zeros_like(temb_ref)
    for s in range(x_ref.shape[0] // L):
        temb_ref[s : s + 1, :] = jnp.sum(gt_ref[s * L : (s + 1) * L, :], axis=0, keepdims=True)


def time_features(timesteps, width):
    half = width // 2
    frequency = jnp.exp(-math.log(10000.0) * jnp.arange(half, dtype=F32) / half)
    angles = timesteps.astype(F32)[:, None] * frequency[None, :]
    return jnp.concatenate([jnp.cos(angles), jnp.sin(angles)], axis=1)


def swap(value, axis, size, bit):
    return lax.ppermute(value, axis, [(i, i ^ bit) for i in range(size)])


def halves(bit_set, mine, other):
    low = jnp.where(bit_set, other, mine)
    high = jnp.where(bit_set, mine, other)
    return low, high


def local(dp, tensor, *args):
    (
        tokens, timesteps, lengths, time_inner, time_ibias, time_outer, time_obias, qkv_weight,
        qv_bias, out_weight, out_bias, gain_first, shift_first, up_weight, up_bias, down_weight,
        down_bias, gain_second, shift_second, cotangent,
    ) = args
    rows, width = tokens.shape
    seqs = rows // L
    w = qkv_weight.shape[2]
    hid = up_weight.shape[0]
    t = lax.axis_index("tensor")
    d = lax.axis_index("dp")
    bits = [1 << i for i in range(dp.bit_length() - 1)]
    core = lambda v: swap(v, "tensor", tensor, 1)
    across = lambda v: swap(v, "tensor", tensor, 2)
    odd = (d & 1) == 1

    flat_qkv = jnp.transpose(qkv_weight, (1, 2, 0)).reshape(3 * w, width)
    pad = lambda v, lo: jnp.pad(v, (lo, width - lo - v.shape[0]))
    bias_rows = jnp.stack(
        [pad(qv_bias[0], 0), pad(qv_bias[0], w), pad(qv_bias[1], 0), pad(qv_bias[1], w), up_bias]
        + [jnp.zeros((width,), BF)] * 11
    )
    wa = jnp.concatenate([flat_qkv, out_weight, bias_rows], axis=0)
    part = 2 * w
    wa_core = core(wa)
    wa_y = across(
        jnp.concatenate(
            [jnp.where(odd, wa[part : 2 * part], wa[:part]), bias_rows], axis=0
        )
    )
    wa_x = swap(wa_y[:part], "dp", dp, 1)
    lo_part, hi_part = halves(odd, wa_y[:part], wa_x)
    wa_far = jnp.concatenate([lo_part, hi_part, wa_y[part:]], axis=0)
    wa_far2 = core(wa_far)
    up_core, down_core = core(up_weight), core(down_weight)
    ffn_y = across(jnp.where(odd, down_weight, up_weight))
    ffn_x = swap(ffn_y, "dp", dp, 1)
    up_far, down_far = halves(odd, ffn_y, ffn_x)
    up_far2, down_far2 = core(up_far), core(down_far)

    features = time_features(timesteps, time_inner.shape[0])
    touter = time_outer.astype(F32)
    tinner = time_inner.astype(F32)
    hidden_time = jax.nn.silu(exact(features, tinner, NN) + time_ibias.astype(F32))
    temb = exact(hidden_time, touter, NN) + time_obias.astype(F32)
    temb = jnp.pad(temb, ((0, 8 - seqs), (0, 0))) if seqs < 8 else temb
    own_len = lax.dynamic_slice(lengths, (t * seqs,), (seqs,))
    vecs = jnp.stack(
        [out_bias, gain_first, shift_first, down_bias, gain_second, shift_second, out_bias, out_bias]
    ).astype(F32)

    wide = 2 * w
    pairs = wide // (2 * HD)
    act_shapes = [
        sds((rows, 3 * wide), BF),
        sds((seqs * pairs, 2 * L, L), F32),
        sds((rows, wide), BF),
    ]
    full = sds((rows, width), F32)
    low_full = sds((rows, width), BF)
    attn_flops = 2 * rows * width * 4 * wide + 4 * rows * L * wide
    x, qkv_n, p_n, mix_n, acc_n = call(
        attn_near_body, [low_full] + act_shapes + [full],
        (own_len, tokens, temb, wa, wa_core), attn_flops, smem=(0,),
    )
    qkv_f, p_f, mix_f, first, normed = call(
        attn_far_body, act_shapes + [full, low_full],
        (own_len, tokens, temb, x, wa_far, wa_far2, acc_n, vecs), attn_flops, smem=(0,),
    )
    mlp_shapes = [sds((rows, 2 * hid), BF), sds((rows, 2 * hid), F32)]
    mlp_flops = 2 * rows * width * 4 * hid
    bias_of = lambda v: v[4 * w :]
    b_n, b_nc, b_f, b_fc = bias_of(wa), bias_of(wa_core), bias_of(wa_far), bias_of(wa_far2)
    act_n, slope_n, mlp_n = call(
        mlp_near_body, mlp_shapes + [full],
        (normed, up_weight, up_core, down_weight, down_core, b_n, b_nc), mlp_flops,
    )
    act_f, slope_f, layer_out, g2, sums2 = call(
        mlp_far_body, mlp_shapes + [low_full, full, sds((8, width), F32)],
        (normed, up_far, up_far2, down_far, down_far2, b_f, b_fc, mlp_n, first, vecs, cotangent),
        mlp_flops, scratch=[pltpu.VMEM((rows, width), F32)],
    )
    dw_shapes = [sds((hid, width), F32), sds((hid, width), BF)] * 2
    duf, duf2, ddf, ddf2, bup_f, gn_f = call(
        mlp_bwd_far_body, dw_shapes + [sds((8, hid), F32), full],
        (normed, g2, up_far, up_far2, down_far, down_far2, act_f, slope_f), 2 * mlp_flops,
    )
    f_far = jnp.concatenate([duf + core(duf2), ddf + core(ddf2)], axis=0).astype(BF)
    f_y = across(f_far)
    dun, dun2, ddn, ddn2, bup_n, g1, sums1 = call(
        mlp_bwd_near_body, dw_shapes + [sds((8, hid), F32), full, sds((8, width), F32)],
        (normed, g2, up_weight, up_core, down_weight, down_core, act_n, slope_n, gn_f, first, vecs),
        2 * mlp_flops,
    )
    f_own = jnp.concatenate([dun + core(dun2), ddn + core(ddn2)], axis=0) + f_y
    da_shapes = [sds((4 * w, width), F32), sds((4 * w, width), BF), sds((8, wide), F32)]
    bwd_scratch = [pltpu.VMEM((rows, wide), BF), pltpu.VMEM((rows, 3 * wide), BF)]
    daf, daf2, qvb_f, gin_f = call(
        attn_bwd_far_body, da_shapes + [full],
        (x, g1, wa_far, wa_far2, qkv_f, p_f, mix_f), 2 * attn_flops, scratch=bwd_scratch,
    )
    a_y = across((daf + core(daf2)).astype(BF))
    dan, dan2, qvb_n, grad_tokens, gtemb = call(
        attn_bwd_near_body, da_shapes + [full, sds((8, width), F32)],
        (x, g1, wa, wa_core, qkv_n, p_n, mix_n, gin_f), 2 * attn_flops, scratch=bwd_scratch,
    )
    a_own = dan + core(dan2) + a_y

    def reduce_dp(value):
        for bit in bits:
            h = value.shape[0] // 2
            up = (d & bit) != 0
            send = jnp.where(up, value[:h], value[h:]).astype(BF)
            keep = jnp.where(up, value[h:], value[:h])
            value = keep + swap(send, "dp", dp, bit).astype(F32)
        value = value.astype(BF)
        for bit in bits[::-1]:
            other = swap(value, "dp", dp, bit)
            low, high = halves((d & bit) != 0, value, other)
            value = jnp.concatenate([low, high], axis=0)
        return value.astype(F32)

    f_all = reduce_dp(f_own)
    a_all = reduce_dp(a_own)

    slot = jnp.arange(tensor, dtype=jnp.int32)
    qv_row = lambda s, at: jnp.concatenate([s[0, at * w : (at + 1) * w], s[1, at * w : (at + 1) * w]])
    rel = [
        (bup_n[0], qv_row(qvb_n, 0)), (bup_n[1], qv_row(qvb_n, 1)),
        (bup_f[0], qv_row(qvb_f, 0)), (bup_f[1], qv_row(qvb_f, 1)),
    ]
    bup_rows = 0.0
    qv_rows = 0.0
    for r, (bu, qv) in enumerate(rel):
        here = (slot == (t ^ r))[:, None]
        bup_rows = bup_rows + jnp.where(here, bu[None, :], 0.0)
        qv_rows = qv_rows + jnp.where(here, jnp.pad(qv, (0, width - 2 * w))[None, :], 0.0)
    small = jnp.concatenate([sums2[:3], sums1[:3], bup_rows, qv_rows], axis=0)
    gath = gtemb[:seqs]
    hops = [("tensor", tensor, 1), ("tensor", tensor, 2)] + [("dp", dp, bit) for bit in bits]
    for axis, size, bit in hops:
        n = small.shape[0]
        other = swap(jnp.concatenate([small, gath], axis=0), axis, size, bit)
        small = small + other[:n]
        me = t if axis == "tensor" else d
        low, high = halves((me & bit) != 0, gath, other[n:])
        gath = jnp.concatenate([low, high], axis=0)
    all_steps = lax.all_gather(timesteps, ("dp", "tensor"), axis=0, tiled=True)
    feats = time_features(all_steps, time_inner.shape[0])
    pre = exact(feats, tinner, NN) + time_ibias.astype(F32)
    act_t, silu_back = jax.vjp(jax.nn.silu, pre)
    grad_touter = exact(act_t, gath, TN)
    grad_tobias = jnp.sum(gath, axis=0)
    grad_hidden = silu_back(exact(gath, touter, NT))[0]
    grad_tinner = exact(feats, grad_hidden, TN)
    grad_tibias = jnp.sum(grad_hidden, axis=0)

    grad_qkv = jnp.transpose(a_all[: 3 * w].reshape(3, w, width), (2, 0, 1))
    own_bup = lax.dynamic_slice(small, (6 + t, 0), (1, width))[0]
    own_qv = lax.dynamic_slice(small, (6 + tensor + t, 0), (1, width))[0, : 2 * w].reshape(2, w)
    return (
        layer_out,
        grad_tokens,
        grad_tinner,
        grad_tibias,
        grad_touter,
        grad_tobias,
        grad_qkv,
        own_qv,
        a_all[3 * w :],
        small[5],
        small[3],
        small[4],
        f_all[:hid],
        own_bup,
        f_all[hid:],
        small[2],
        small[0],
        small[1],
    )


def solution(mesh):
    both = ("dp", "tensor")
    placed = (
        P(both, None), P(both), P("dp"), P(), P(), P(), P(), P(None, None, "tensor"),
        P(None, "tensor"), P("tensor", None), P(), P(), P(), P("tensor", None), P("tensor"),
        P("tensor", None), P(), P(), P(), P(both, None),
    )
    return jax.shard_map(
        functools.partial(local, mesh.shape["dp"], mesh.shape["tensor"]),
        mesh=mesh,
        in_specs=placed,
        out_specs=(
            P(both, None), P(both, None), P(), P(), P(), P(), P(None, None, "tensor"),
            P(None, "tensor"), P("tensor", None), P(), P(), P(), P("tensor", None), P("tensor"),
            P("tensor", None), P(), P(), P(),
        ),
        check_vma=False,
    )
```

time: 1000 us -> 497 us (0.50)
  waiting for transfers between devices: 710 us -> 237 us
  Pallas kernels: 0 us -> 117 us
  matrix products: 117 us -> 6.43 us
  starting transfers between devices: 1.42 us -> 30.9 us
  blocking collectives: 63.9 us -> 40.7 us
  local copies, waits for them, and re-layouts: 47.2 us -> 27.2 us
  between operations: 15.3 us -> 1.99 us
    psum x2 -> x0, waiting for transfers between devices: 308 us -> none  [the longest x1 170 us: local(): lax.psum((grad_qkv, grad_qvbias, grad_wout, grad_wup, grad_bup, grad_wdow...]
    reduce_scatter x4 -> x0, waiting for transfers between devices: 251 us -> none  [the longest x1 78.5 us: local(): lax.psum_scatter(direct(grad_pre, up_weight, normal_dims), 'tensor', scat...]
    ppermute x0 -> x35, waiting for transfers between devices: none -> 237 us  [swap(): return lax.ppermute(value, axis, [(i, i ^ bit) for i in range(size)])]
    all_gather x4 -> x0, waiting for transfers between devices: 151 us -> none  [the longest x1 40 us: local(): start_all = lax.all_gather(start_low, 'tensor', axis=0, tiled=True)]
    pallas_call x0 -> x8, Pallas kernels: none -> 117 us  [call(): pl.pallas_call(body, out_shape=outs, in_specs=[pl.BlockSpec(memory_space=...]
    dot_general x19 -> x0, matrix products: 110 us -> none  [the longest x12 95 us: direct(): lax.dot_general(left, right, (dims, ((), ())), preferred_element_type=jnp...]
    psum x2 -> x0, blocking collectives: 63.9 us -> none  [the longest x1 40.7 us: local(): lax.psum((grad_tinner, grad_tibias, grad_touter, grad_tobias, grad_bout,...]
    unnamed x0 -> x1, blocking collectives: none -> 40.7 us
  transfers between devices with their start and end apart: 10 -> 35, of which waited for: 10 -> 15; matrix products, arithmetic and copies ran while one was open for 4% -> 9% of each run, Pallas kernels for 0% -> 8%
where the time goes in v1:
time: 497 us; the launch traced here: 490 us
  waiting for transfers between devices  237 us (48%)
  Pallas kernels  117 us (24%)
  blocking collectives  40.7 us (8%)
  starting transfers between devices  30.9 us (6%)
  other arithmetic  29.9 us (6%)
  local copies, waits for them, and re-layouts  27.2 us (5%)
  matrix products  6.43 us (1%)
    ppermute x35, waiting for transfers between devices, swap(): return lax.ppermute(value, axis, [(i, i ^ bit) for i in range(size)])  237 us
    pallas_call x8, Pallas kernels, call(): pl.pallas_call(body, out_shape=outs, in_specs=[pl.BlockSpec(memory_space=...  117 us
    unnamed x1, blocking collectives  40.7 us
    ppermute x35, starting transfers between devices, swap(): return lax.ppermute(value, axis, [(i, i ^ bit) for i in range(size)])  30.9 us
  transfers between devices with their start and end apart: 35, of which 15 were waited for; matrix products, arithmetic and copies ran while one was open for 9% of the time, Pallas kernels for 8%

profile of v1, /device:TPU:0, one launch (start us, length us, event | category | flops | bytes accessed | tf_op | source)
XLA Modules:
  0.0 490.4 jit_solution(2711309545988850350)
XLA Ops:
  0.7 2.5 broadcast_select_fusion.4
  3.2 3.0 collective-permute-start.4
  7.8 37.7 %collective-permute-done.1 = bf16[400,768]{1,0:T(8,128)(2,1)S(1)} collective-permute-done((bf16[400,768]{1,0:T(8,128)(2,1)S(1)}, bf16[400,768]{1,0:T(8,128)(2,1)S(1)}, u32[]{:S(2)}, u32[]{:S(2)}) %collective-permute-start.1) | collective-permute-done | bytes 614432 | tf_op jit(solution)/shard_map/ppermute | solution.py:366
  46.4 1.7 collective-permute-start.2
  49.0 2.1 concatenate.96.a_ref
  51.3 11.6 %collective-permute-done.2 = bf16[384,768]{1,0:T(8,128)(2,1)} collective-permute-done((bf16[384,768]{1,0:T(8,128)(2,1)}, bf16[384,768]{1,0:T(8,128)(2,1)}, u32[]{:S(2)}, u32[]{:S(2)}) %collective-permute-start.2) | collective-permute-done | bytes 589856 | tf_op jit(solution)/shard_map/ppermute | solution.py:366
  68.2 18.3 %collective-permute-done.5 = bf16[768,768]{1,0:T(8,128)(2,1)} collective-permute-done((bf16[768,768]{1,0:T(8,128)(2,1)}, bf16[768,768]{1,0:T(8,128)(2,1)}, u32[]{:S(2)}, u32[]{:S(2)}) %collective-permute-start.5) | collective-permute-done | bytes 1179680 | tf_op jit(solution)/shard_map/ppermute | solution.py:366
  86.5 1.8 broadcast_select_fusion.2
  91.3 10.9 %shard_map.331 = (bf16[768,768]{1,0:T(8,128)(2,1)}, bf16[768,1152]{1,0:T(8,128)(2,1)}, f32[18,256,128]{2,1,0:T(8,128)}, bf16[768,384]{1,0:T(8,128)(2,1)}, f32[768,768]{1,0:T(8,128)}) custom-call(s32[6]{0:T(128)} %dynamic_slice.9.len_ref, bf16[768,768]{1,0:T(8,128)(2,1)} %tok_ref.3, f32[8,768]{1,0:T(8,128)} %pad.31.temb_ref, bf16[784,768]{1,0:T(8,128)(2,1)} %copy-done.10, ...), custom_call_target="tpu_custom_call" | custom-call | flops 1962934272 | bytes 11870232 | tf_op jit(solution)/shard_map/pallas_call | solution.py:35
  103.6 13.4 %shard_map.332 = (bf16[768,1152]{1,0:T(8,128)(2,1)}, f32[18,256,128]{2,1,0:T(8,128)}, bf16[768,384]{1,0:T(8,128)(2,1)}, f32[768,768]{1,0:T(8,128)}, bf16[768,768]{1,0:T(8,128)(2,1)}) custom-call(s32[6]{0:T(128)} %dynamic_slice.9.len_ref, bf16[768,768]{1,0:T(8,128)(2,1)} %tok_ref.3, f32[8,768]{1,0:T(8,128)} %pad.31.temb_ref, ...), custom_call_target="tpu_custom_call" | custom-call | flops 1962934272 | bytes 15433752 | tf_op jit(solution)/shard_map/pallas_call | solution.py:35
  117.0 12.7 %shard_map.333 = (bf16[768,1536]{1,0:T(8,128)(2,1)}, f32[768,1536]{1,0:T(8,128)}, f32[768,768]{1,0:T(8,128)}) custom-call(bf16[768,768]{1,0:T(8,128)(2,1)} %get-tuple-element.60.x_ref, bf16[768,768]{1,0:T(8,128)(2,1)} %ua.3, bf16[768,768]{1,0:T(8,128)(2,1)} %collective-permute-done.8.ub, bf16[768,768]{1,0:T(8,128)(2,1)} %da.3, ...), custom_call_target="tpu_custom_call" | custom-call | flops 3623878656 | bytes 15384576 | tf_op jit(solution)/shard_map/pallas_call | solution.py:35
  131.1 16.2 %shard_map.334 = (bf16[768,1536]{1,0:T(8,128)(2,1)}, f32[768,1536]{1,0:T(8,128)}, bf16[768,768]{1,0:T(8,128)(2,1)}, f32[768,768]{1,0:T(8,128)}, f32[8,768]{1,0:T(8,128)}) custom-call(bf16[768,768]{1,0:T(8,128)(2,1)} %get-tuple-element.60.x_ref, bf16[768,768]{1,0:T(8,128)(2,1)} %copy-done.13, bf16[768,768]{1,0:T(8,128)(2,1)} %copy-done.35, ...), custom_call_target="tpu_custom_call" | custom-call | flops 3623878656 | bytes 22511616 | tf_op jit(solution)/shard_map/pallas_call | solution.py:35
  148.0 14.6 %shard_map.335 = (f32[768,768]{1,0:T(8,128)}, bf16[768,768]{1,0:T(8,128)(2,1)}, f32[768,768]{1,0:T(8,128)}, bf16[768,768]{1,0:T(8,128)(2,1)}, f32[8,768]{1,0:T(8,128)}, /*index=5*/f32[768,768]{1,0:T(8,128)}) custom-call(bf16[768,768]{1,0:T(8,128)(2,1)} %get-tuple-element.60.x_ref, f32[768,768]{1,0:T(8,128)} %get-tuple-element.64.g_ref, ...), custom_call_target="tpu_custom_call" | custom-call | flops 7247757312 | bytes 24797184 | tf_op jit(solution)/shard_map/pallas_call | solution.py:35
  162.5 17.1 %shard_map.336 = (f32[768,768]{1,0:T(8,128)}, bf16[768,768]{1,0:T(8,128)(2,1)}, f32[768,768]{1,0:T(8,128)}, bf16[768,768]{1,0:T(8,128)(2,1)}, f32[8,768]{1,0:T(8...) custom-call(bf16[768,768]{1,0:T(8,128)(2,1)} %get-tuple-element.60.x_ref, f32[768,768]{1,0:T(8,128)} %get-tuple-element.64.g_ref, ...), custom_call_target="tpu_custom_call" | custom-call | flops 7247757312 | bytes 29564928 | tf_op jit(solution)/shard_map/pallas_call | solution.py:35
  180.4 15.5 %shard_map.337 = (f32[768,768]{1,0:T(8,128)}, bf16[768,768]{1,0:T(8,128)(2,1)}, f32[8,384]{1,0:T(8,128)}, f32[768,768]{1,0:T(8,128)}) custom-call(bf16[768,768]{1,0:T(8,128)(2,1)} %get-tuple-element.58.x_ref, f32[768,768]{1,0:T(8,128)} %get-tuple-element.70.g_ref, bf16[784,768]{1,0:T(8,128)(2,1)} %pad_maximum_fusion.1.a_ref, ...), custom_call_target="tpu_custom_call" | custom-call | flops 3925868544 | bytes 16576512 | tf_op jit(solution)/shard_map/pallas_call | solution.py:35
  196.8 16.3 %shard_map.338 = (f32[768,768]{1,0:T(8,128)}, bf16[768,768]{1,0:T(8,128)(2,1)}, f32[8,384]{1,0:T(8,128)}, f32[768,768]{1,0:T(8,128)}, f32[8,768]{1,0:T(8,128)}) custom-call(bf16[768,768]{1,0:T(8,128)(2,1)} %get-tuple-element.58.x_ref, f32[768,768]{1,0:T(8,128)} %get-tuple-element.70.g_ref, bf16[784,768]{1,0:T(8,128)(2,1)} %copy-done.10, ...), custom_call_target="tpu_custom_call" | custom-call | flops 3925868544 | bytes 18960384 | tf_op jit(solution)/shard_map/pallas_call | solution.py:35
  217.4 40.7 %all-reduce.9 = s32[192]{0:T(256)S(1)} all-reduce(s32[192]{0:T(256)S(1)} %dynamic-update-slice), channel_id=1, replica_groups=mesh['dp'=8,'tensor'=4] {'dp','tensor'}, use_global_device_ids=true, to_apply=%add.9 | all-reduce | flops 192 | bytes 1536
  259.5 2.3 collective-permute-start.11
  263.4 1.4 collective-permute-done.11
  265.5 1.7 add_convert_fusion
  267.5 1.5 add_convert_fusion.1
  269.2 1.8 collective-permute-start.28
  272.0 4.1 collective-permute-done.12
  277.1 1.5 collective-permute-start.13
  278.9 1.4 copy-done.8
  280.6 67.1 %collective-permute-done.17 = bf16[768,768]{1,0:T(8,128)(2,1)S(1)} collective-permute-done((bf16[768,768]{1,0:T(8,128)(2,1)S(1)}, bf16[768,768]{1,0:T(8,128)(2,1)S(1)}, u32[]{:S(2)}, u32[]{:S(2)}) %collective-permute-start.17) | collective-permute-done | bytes 1179680 | tf_op jit(solution)/shard_map/ppermute | solution.py:366
  349.0 1.7 collective-permute-start.18
  351.2 2.2 copy-done.1
  357.2 2.4 collective-permute-start.14
  359.6 6.0 %collective-permute-done.18 = bf16[384,768]{1,0:T(8,128)(2,1)} collective-permute-done((bf16[384,768]{1,0:T(8,128)(2,1)}, bf16[384,768]{1,0:T(8,128)(2,1)}, u32[]{:S(2)}, u32[]{:S(2)}) %collective-permute-start.18) | collective-permute-done | bytes 589856 | tf_op jit(solution)/shard_map/ppermute | solution.py:366
  367.1 1.6 collective-permute-start.19
  368.6 20.4 %collective-permute-done.29 = bf16[768,768]{1,0:T(8,128)(2,1)} collective-permute-done((bf16[768,768]{1,0:T(8,128)(2,1)}, bf16[768,768]{1,0:T(8,128)(2,1)}, u32[]{:S(2)}, u32[]{:S(2)}) %collective-permute-start.29) | collective-permute-done | bytes 1179680 | tf_op jit(solution)/shard_map/ppermute | solution.py:366
  389.0 1.6 convert_add_fusion
  390.8 1.6 collective-permute-start.30
  394.5 13.0 %collective-permute-done.30 = bf16[384,768]{1,0:T(8,128)(2,1)S(1)} collective-permute-done((bf16[384,768]{1,0:T(8,128)(2,1)S(1)}, bf16[384,768]{1,0:T(8,128)(2,1)S(1)}, u32[]{:S(2)}, u32[]{:S(2)}) %collective-permute-start.30) | collective-permute-done | bytes 589856 | tf_op jit(solution)/shard_map/ppermute | solution.py:366
  412.1 2.2 collective-permute-start.21
  414.3 10.9 %collective-permute-done.31 = bf16[192,768]{1,0:T(8,128)(2,1)} collective-permute-done((bf16[192,768]{1,0:T(8,128)(2,1)}, bf16[192,768]{1,0:T(8,128)(2,1)}, u32[]{:S(2)}, u32[]{:S(2)}) %collective-permute-start.31) | collective-permute-done | bytes 294944 | tf_op jit(solution)/shard_map/ppermute | solution.py:366
  426.4 6.1 %collective-permute-done.21 = bf16[96,768]{1,0:T(8,128)(2,1)S(1)} collective-permute-done((bf16[96,768]{1,0:T(8,128)(2,1)S(1)}, bf16[96,768]{1,0:T(8,128)(2,1)S(1)}, u32[]{:S(2)}, u32[]{:S(2)}) %collective-permute-start.21) | collective-permute-done | bytes 147488 | tf_op jit(solution)/shard_map/ppermute | solution.py:366
  432.6 8.3 %collective-permute-done.32 = bf16[192,768]{1,0:T(8,128)(2,1)S(1)} collective-permute-done((bf16[192,768]{1,0:T(8,128)(2,1)S(1)}, bf16[192,768]{1,0:T(8,128)(2,1)S(1)}, u32[]{:S(2)}, u32[]{:S(2)}) %collective-permute-start.32) | collective-permute-done | bytes 294944 | tf_op jit(solution)/shard_map/ppermute | solution.py:366
  441.2 1.6 fusion.31
  442.7 4.2 collective-permute-done.22
  447.1 1.8 collective-permute-start.23
  448.9 10.0 %collective-permute-done.33 = bf16[384,768]{1,0:T(8,128)(2,1)S(1)} collective-permute-done((bf16[384,768]{1,0:T(8,128)(2,1)S(1)}, bf16[384,768]{1,0:T(8,128)(2,1)S(1)}, u32[]{:S(2)}, u32[]{:S(2)}) %collective-permute-start.33) | collective-permute-done | bytes 589856 | tf_op jit(solution)/shard_map/ppermute | solution.py:366
  459.3 1.8 collective-permute-start.34
  461.1 1.7 slice_reduce_fusion
  464.0 2.6 fusion.1
  469.2 17.4 %collective-permute-done.34 = bf16[768,768]{1,0:T(8,128)(2,1)S(1)} collective-permute-done((bf16[768,768]{1,0:T(8,128)(2,1)S(1)}, bf16[768,768]{1,0:T(8,128)(2,1)S(1)}, u32[]{:S(2)}, u32[]{:S(2)}) %collective-permute-start.34) | collective-permute-done | bytes 1179680 | tf_op jit(solution)/shard_map/ppermute | solution.py:366
  487.5 2.5 fusion.26
  (225 shorter events, 47.8 us)
Async XLA Ops:
  0.7 88.3 %copy-start = (bf16[512,768]{1,0:T(8,128)(2,1)S(1)}, bf16[512,768]{1,0:T(8,128)(2,1)}, u32[]{:S(2)}) copy-start(bf16[512,768]{1,0:T(8,128)(2,1)} %param.25) | copy-start | bytes 2359300
  0.7 5.5 %copy-start.25 = (bf16[2,192]{1,0:T(2,128)(2,1)S(1)}, bf16[2,192]{1,0:T(2,128)(2,1)}, u32[]{:S(2)}) copy-start(bf16[2,192]{1,0:T(2,128)(2,1)} %param.28) | copy-start | bytes 2308
  0.7 5.7 %copy-start.27 = (bf16[768]{0:T(1024)(128)(2,1)S(1)}, bf16[768]{0:T(1024)(128)(2,1)}, u32[]{:S(2)}) copy-start(bf16[768]{0:T(1024)(128)(2,1)} %param.34) | copy-start | bytes 4612
  0.7 5.7 %copy-start.3 = (bf16[768,3,192]{0,2,1:T(8,128)(2,1)S(1)}, bf16[768,3,192]{0,2,1:T(8,128)(2,1)}, u32[]{:S(2)}) copy-start(bf16[768,3,192]{0,2,1:T(8,128)(2,1)} %param.27) | copy-start | bytes 2654212
  3.2 44.9 %collective-permute-start.4 = (bf16[768,768]{1,0:T(8,128)(2,1)}, bf16[768,768]{1,0:T(8,128)(2,1)}, u32[]{:S(2)}, u32[]{:S(2)}) collective-permute-start(bf16[768,768]{1,0:T(8,128)(2,1)} %broadcast_select_fusion.4), channel_id=1, source_target_pairs={{0,2},{1,3},{2,0},{3,1},{4,6},{5,7},{6,4},{7,5},{8,10},{9,11},{10,... | collective-permute-start | bytes 3538952 | tf_op jit(solution)/shard_map/ppermute | solution.py:366
  7.0 38.5 %collective-permute-start.1 = (bf16[400,768]{1,0:T(8,128)(2,1)S(1)}, bf16[400,768]{1,0:T(8,128)(2,1)S(1)}, u32[]{:S(2)}, u32[]{:S(2)}) collective-permute-start(bf16[400,768]{1,0:T(8,128)(2,1)S(1)} %concatenate.98), channel_id=1, source_target_pairs={{0,2},{1,3},{2,0},{3,1},{4,6},{5,7},{6,4},{7,5},{8,10},{9,11},{10,... | collective-permute-start | bytes 1843208 | tf_op jit(solution)/shard_map/ppermute | solution.py:366
  46.4 4.8 copy-start.38
  46.4 16.6 %collective-permute-start.2 = (bf16[384,768]{1,0:T(8,128)(2,1)}, bf16[384,768]{1,0:T(8,128)(2,1)}, u32[]{:S(2)}, u32[]{:S(2)}) collective-permute-start(bf16[384,768]{1,0:T(8,128)(2,1)} %slice.245), channel_id=1, source_target_pairs={{0,4},{4,0},{8,12},{12,8},{16,20},{20,16},{24,28},{28,24},{1,5},{5... | collective-permute-start | bytes 1769480 | tf_op jit(solution)/shard_map/ppermute | solution.py:366
  48.1 38.4 %collective-permute-start.5 = (bf16[768,768]{1,0:T(8,128)(2,1)}, bf16[768,768]{1,0:T(8,128)(2,1)}, u32[]{:S(2)}, u32[]{:S(2)}) collective-permute-start(bf16[768,768]{1,0:T(8,128)(2,1)} %collective-permute-done.4), channel_id=1, source_target_pairs={{0,4},{4,0},{8,12},{12,8},{16,20},{20,16},{24,28},{28,24},{1,5},{5... | collective-permute-start | bytes 3538952 | tf_op jit(solution)/shard_map/ppermute | solution.py:366
  48.4 68.5 %collective-permute-start.8 = (bf16[768,768]{1,0:T(8,128)(2,1)}, bf16[768,768]{1,0:T(8,128)(2,1)}, u32[]{:S(2)}, u32[]{:S(2)}) collective-permute-start(bf16[768,768]{1,0:T(8,128)(2,1)} %ua.3), channel_id=1, source_target_pairs={{0,1},{1,0},{2,3},{3,2},{4,5},{5,4},{6,7},{7,6},{8,9},{9,8},{10,11... | collective-permute-start | bytes 3538952 | tf_op jit(solution)/shard_map/ppermute | solution.py:366
  48.4 68.5 %collective-permute-start.9 = (bf16[768,768]{1,0:T(8,128)(2,1)}, bf16[768,768]{1,0:T(8,128)(2,1)}, u32[]{:S(2)}, u32[]{:S(2)}) collective-permute-start(bf16[768,768]{1,0:T(8,128)(2,1)} %da.3), channel_id=1, source_target_pairs={{0,1},{1,0},{2,3},{3,2},{4,5},{5,4},{6,7},{7,6},{8,9},{9,8},{10,11... | collective-permute-start | bytes 3538952 | tf_op jit(solution)/shard_map/ppermute | solution.py:366
  51.1 13.1 %copy-start.10 = (bf16[784,768]{1,0:T(8,128)(2,1)}, bf16[784,768]{1,0:T(8,128)(2,1)S(1)}, u32[]{:S(2)}) copy-start(bf16[784,768]{1,0:T(8,128)(2,1)S(1)} %concatenate.96.a_ref) | copy-start | bytes 3612676
  51.1 37.3 %collective-permute-start = (bf16[784,768]{1,0:T(8,128)(2,1)S(1)}, bf16[784,768]{1,0:T(8,128)(2,1)}, u32[]{:S(2)}, u32[]{:S(2)}) collective-permute-start(bf16[784,768]{1,0:T(8,128)(2,1)S(1)} %concatenate.96.a_ref), channel_id=1, source_target_pairs={{0,1},{1,0},{2,3},{3,2},{4,5},{5,4},{6,7},{7,6},{8,9},{9,8},{10,11... | collective-permute-start | bytes 3612680 | tf_op jit(solution)/shard_map/ppermute | solution.py:366
  51.3 14.0 %copy-start.24 = (bf16[16,768]{1,0:T(8,128)(2,1)}, bf16[16,768]{1,0:T(8,128)(2,1)S(1)}, u32[]{:S(2)}) copy-start(bf16[16,768]{1,0:T(8,128)(2,1)S(1)} %slice.246.ba) | copy-start | bytes 73732
  65.4 36.9 %collective-permute-start.3 = (bf16[784,768]{1,0:T(8,128)(2,1)}, bf16[784,768]{1,0:T(8,128)(2,1)}, u32[]{:S(2)}, u32[]{:S(2)}) collective-permute-start(bf16[784,768]{1,0:T(8,128)(2,1)} %pad_maximum_fusion.1.a_ref), channel_id=1, source_target_pairs={{0,1},{1,0},{2,3},{3,2},{4,5},{5,4},{6,7},{7,6},{8,9},{9,8},{10,11... | collective-permute-start | bytes 3612680 | tf_op jit(solution)/shard_map/ppermute | solution.py:366
  88.3 13.9 %copy-start.12 = (bf16[768,768]{1,0:T(8,128)(2,1)}, bf16[768,768]{1,0:T(8,128)(2,1)S(1)}, u32[]{:S(2)}) copy-start(bf16[768,768]{1,0:T(8,128)(2,1)S(1)} %get-tuple-element.119.da) | copy-start | bytes 3538948
  88.3 13.9 %copy-start.13 = (bf16[768,768]{1,0:T(8,128)(2,1)}, bf16[768,768]{1,0:T(8,128)(2,1)S(1)}, u32[]{:S(2)}) copy-start(bf16[768,768]{1,0:T(8,128)(2,1)S(1)} %get-tuple-element.120.ua) | copy-start | bytes 3538948
  88.3 41.3 %collective-permute-start.6 = (bf16[768,768]{1,0:T(8,128)(2,1)S(1)}, bf16[768,768]{1,0:T(8,128)(2,1)S(1)}, u32[]{:S(2)}, u32[]{:S(2)}) collective-permute-start(bf16[768,768]{1,0:T(8,128)(2,1)S(1)} %get-tuple-element.120.ua), channel_id=1, source_target_pairs={{0,1},{1,0},{2,3},{3,2},{4,5},{5,4},{6,7},{7,6},{8,9},{9,8},{10,11... | collective-permute-start | bytes 3538952 | tf_op jit(solution)/shard_map/ppermute | solution.py:366
  88.4 41.3 %collective-permute-start.7 = (bf16[768,768]{1,0:T(8,128)(2,1)S(1)}, bf16[768,768]{1,0:T(8,128)(2,1)S(1)}, u32[]{:S(2)}, u32[]{:S(2)}) collective-permute-start(bf16[768,768]{1,0:T(8,128)(2,1)S(1)} %get-tuple-element.119.da), channel_id=1, source_target_pairs={{0,1},{1,0},{2,3},{3,2},{4,5},{5,4},{6,7},{7,6},{8,9},{9,8},{10,11... | collective-permute-start | bytes 3538952 | tf_op jit(solution)/shard_map/ppermute | solution.py:366
  196.8 68.7 %copy-start.6 = (f32[768,768]{1,0:T(8,128)S(1)}, f32[768,768]{1,0:T(8,128)}, u32[]{:S(2)}) copy-start(f32[768,768]{1,0:T(8,128)} %get-tuple-element.96) | copy-start | bytes 7077892
  217.1 41.6 %collective-permute-start.10 = (f32[20,768]{1,0:T(8,128)S(1)}, f32[20,768]{1,0:T(8,128)S(1)}, u32[]{:S(2)}, u32[]{:S(2)}) collective-permute-start(f32[20,768]{1,0:T(8,128)S(1)} %concatenate.106), channel_id=1, source_target_pairs={{0,1},{1,0},{2,3},{3,2},{4,5},{5,4},{6,7},{7,6},{8,9},{9,8},{10,11... | collective-permute-start | bytes 184328 | tf_op jit(solution)/shard_map/ppermute | solution.py:366
  258.1 6.8 %collective-permute-start.27 = (bf16[768,768]{1,0:T(8,128)(2,1)}, bf16[768,768]{1,0:T(8,128)(2,1)}, u32[]{:S(2)}, u32[]{:S(2)}) collective-permute-start(bf16[768,768]{1,0:T(8,128)(2,1)} %get-tuple-element.97), channel_id=1, source_target_pairs={{0,1},{1,0},{2,3},{3,2},{4,5},{5,4},{6,7},{7,6},{8,9},{9,8},{10,11... | collective-permute-start | bytes 3538952 | tf_op jit(solution)/shard_map/ppermute | solution.py:366
  258.2 9.0 %collective-permute-start.26 = (bf16[768,768]{1,0:T(8,128)(2,1)}, bf16[768,768]{1,0:T(8,128)(2,1)}, u32[]{:S(2)}, u32[]{:S(2)}) collective-permute-start(bf16[768,768]{1,0:T(8,128)(2,1)} %get-tuple-element.95), channel_id=1, source_target_pairs={{0,1},{1,0},{2,3},{3,2},{4,5},{5,4},{6,7},{7,6},{8,9},{9,8},{10,11... | collective-permute-start | bytes 3538952 | tf_op jit(solution)/shard_map/ppermute | solution.py:366
  259.5 5.4 %collective-permute-start.11 = (f32[26,768]{1,0:T(8,128)S(1)}, f32[26,768]{1,0:T(8,128)S(1)}, u32[]{:S(2)}, u32[]{:S(2)}) collective-permute-start(f32[26,768]{1,0:T(8,128)S(1)} %pad_maximum_fusion.18), channel_id=1, source_target_pairs={{0,2},{1,3},{2,0},{3,1},{4,6},{5,7},{6,4},{7,5},{8,10},{9,11},{10,... | collective-permute-start | bytes 239624 | tf_op jit(solution)/shard_map/ppermute | solution.py:366
  262.9 8.1 %collective-permute-start.16 = (bf16[768,768]{1,0:T(8,128)(2,1)}, bf16[768,768]{1,0:T(8,128)(2,1)S(1)}, u32[]{:S(2)}, u32[]{:S(2)}) collective-permute-start(bf16[768,768]{1,0:T(8,128)(2,1)} %get-tuple-element.89), channel_id=1, source_target_pairs={{0,1},{1,0},{2,3},{3,2},{4,5},{5,4},{6,7},{7,6},{8,9},{9,8},{10,11... | collective-permute-start | bytes 3538952 | tf_op jit(solution)/shard_map/ppermute | solution.py:366
  262.9 17.7 %collective-permute-start.15 = (bf16[768,768]{1,0:T(8,128)(2,1)}, bf16[768,768]{1,0:T(8,128)(2,1)S(1)}, u32[]{:S(2)}, u32[]{:S(2)}) collective-permute-start(bf16[768,768]{1,0:T(8,128)(2,1)} %get-tuple-element.87), channel_id=1, source_target_pairs={{0,1},{1,0},{2,3},{3,2},{4,5},{5,4},{6,7},{7,6},{8,9},{9,8},{10,11... | collective-permute-start | bytes 3538952 | tf_op jit(solution)/shard_map/ppermute | solution.py:366
  264.9 12.3 %collective-permute-start.25 = (bf16[768,768]{1,0:T(8,128)(2,1)}, bf16[768,768]{1,0:T(8,128)(2,1)S(1)}, u32[]{:S(2)}, u32[]{:S(2)}) collective-permute-start(bf16[768,768]{1,0:T(8,128)(2,1)} %get-tuple-element.93), channel_id=1, source_target_pairs={{0,1},{1,0},{2,3},{3,2},{4,5},{5,4},{6,7},{7,6},{8,9},{9,8},{10,11... | collective-permute-start | bytes 3538952 | tf_op jit(solution)/shard_map/ppermute | solution.py:366
  264.9 14.0 %collective-permute-start.24 = (bf16[768,768]{1,0:T(8,128)(2,1)}, bf16[768,768]{1,0:T(8,128)(2,1)S(1)}, u32[]{:S(2)}, u32[]{:S(2)}) collective-permute-start(bf16[768,768]{1,0:T(8,128)(2,1)} %get-tuple-element.91), channel_id=1, source_target_pairs={{0,1},{1,0},{2,3},{3,2},{4,5},{5,4},{6,7},{7,6},{8,9},{9,8},{10,11... | collective-permute-start | bytes 3538952 | tf_op jit(solution)/shard_map/ppermute | solution.py:366
  269.2 81.6 %collective-permute-start.28 = (bf16[1536,768]{1,0:T(8,128)(2,1)S(1)}, bf16[1536,768]{1,0:T(8,128)(2,1)S(1)}, u32[]{:S(2)}, u32[]{:S(2)}) collective-permute-start(bf16[1536,768]{1,0:T(8,128)(2,1)S(1)} %pad_maximum_fusion), channel_id=1, source_target_pairs={{0,2},{1,3},{2,0},{3,1},{4,6},{5,7},{6,4},{7,5},{8,10},{9,11},{10,... | collective-permute-start | bytes 7077896 | tf_op jit(solution)/shard_map/ppermute | solution.py:366
  271.0 5.0 %collective-permute-start.12 = (f32[38,768]{1,0:T(8,128)S(1)}, f32[38,768]{1,0:T(8,128)S(1)}, u32[]{:S(2)}, u32[]{:S(2)}) collective-permute-start(f32[38,768]{1,0:T(8,128)S(1)} %pad_maximum_fusion.16), channel_id=1, source_target_pairs={{0,4},{4,0},{8,12},{12,8},{16,20},{20,16},{24,28},{28,24},{1,5},{5... | collective-permute-start | bytes 350216 | tf_op jit(solution)/shard_map/ppermute | solution.py:366
  271.6 7.0 %copy-start.9 = (f32[768,768]{1,0:T(8,128)S(1)}, f32[768,768]{1,0:T(8,128)}, u32[]{:S(2)}) copy-start(f32[768,768]{1,0:T(8,128)} %get-tuple-element.92) | copy-start | bytes 7077892
  276.1 71.6 %collective-permute-start.17 = (bf16[768,768]{1,0:T(8,128)(2,1)S(1)}, bf16[768,768]{1,0:T(8,128)(2,1)S(1)}, u32[]{:S(2)}, u32[]{:S(2)}) collective-permute-start(bf16[768,768]{1,0:T(8,128)(2,1)S(1)} %add_convert_fusion.2), channel_id=1, source_target_pairs={{0,2},{1,3},{2,0},{3,1},{4,6},{5,7},{6,4},{7,5},{8,10},{9,11},{10,... | collective-permute-start | bytes 3538952 | tf_op jit(solution)/shard_map/ppermute | solution.py:366
  277.1 78.2 %collective-permute-start.13 = (f32[62,768]{1,0:T(8,128)}, f32[62,768]{1,0:T(8,128)}, u32[]{:S(2)}, u32[]{:S(2)}) collective-permute-start(f32[62,768]{1,0:T(8,128)} %pad_maximum_fusion.14), channel_id=1, source_target_pairs={{0,8},{4,12},{8,0},{12,4},{16,24},{20,28},{24,16},{28,20},{1,9},{5... | collective-permute-start | bytes 571400 | tf_op jit(solution)/shard_map/ppermute | solution.py:366
  280.3 67.4 %copy-start.4 = (f32[768,768]{1,0:T(8,128)S(1)}, f32[768,768]{1,0:T(8,128)}, u32[]{:S(2)}) copy-start(f32[768,768]{1,0:T(8,128)} %get-tuple-element.86) | copy-start | bytes 7077892
  349.0 16.6 %collective-permute-start.18 = (bf16[384,768]{1,0:T(8,128)(2,1)}, bf16[384,768]{1,0:T(8,128)(2,1)}, u32[]{:S(2)}, u32[]{:S(2)}) collective-permute-start(bf16[384,768]{1,0:T(8,128)(2,1)} %select_convert_fusion.2), channel_id=1, source_target_pairs={{0,4},{4,0},{8,12},{12,8},{16,20},{20,16},{24,28},{28,24},{1,5},{5... | collective-permute-start | bytes 1769480 | tf_op jit(solution)/shard_map/ppermute | solution.py:366
  354.6 34.4 %collective-permute-start.29 = (bf16[768,768]{1,0:T(8,128)(2,1)}, bf16[768,768]{1,0:T(8,128)(2,1)}, u32[]{:S(2)}, u32[]{:S(2)}) collective-permute-start(bf16[768,768]{1,0:T(8,128)(2,1)} %select_convert_fusion), channel_id=1, source_target_pairs={{0,4},{4,0},{8,12},{12,8},{16,20},{20,16},{24,28},{28,24},{1,5},{5... | collective-permute-start | bytes 3538952 | tf_op jit(solution)/shard_map/ppermute | solution.py:366
  357.2 35.1 %collective-permute-start.14 = (f32[110,768]{1,0:T(8,128)S(1)}, f32[110,768]{1,0:T(8,128)S(1)}, u32[]{:S(2)}, u32[]{:S(2)}) collective-permute-start(f32[110,768]{1,0:T(8,128)S(1)} %pad_maximum_fusion.11), channel_id=1, source_target_pairs={{0,16},{4,20},{8,24},{12,28},{16,0},{20,4},{24,8},{28,12},{1,17},{... | collective-permute-start | bytes 1013768 | tf_op jit(solution)/shard_map/ppermute | solution.py:366
  365.6 23.4 %copy-start.2 = (f32[1536,768]{1,0:T(8,128)S(1)}, f32[1536,768]{1,0:T(8,128)}, u32[]{:S(2)}) copy-start(f32[1536,768]{1,0:T(8,128)} %copy-done.1) | copy-start | bytes 14155780
  367.1 25.4 %collective-permute-start.19 = (bf16[192,768]{1,0:T(8,128)(2,1)S(1)}, bf16[192,768]{1,0:T(8,128)(2,1)S(1)}, u32[]{:S(2)}, u32[]{:S(2)}) collective-permute-start(bf16[192,768]{1,0:T(8,128)(2,1)S(1)} %select_convert_fusion.4), channel_id=1, source_target_pairs={{0,8},{4,12},{8,0},{12,4},{16,24},{20,28},{24,16},{28,20},{1,9},{5... | collective-permute-start | bytes 884744 | tf_op jit(solution)/shard_map/ppermute | solution.py:366
  390.8 16.7 %collective-permute-start.30 = (bf16[384,768]{1,0:T(8,128)(2,1)S(1)}, bf16[384,768]{1,0:T(8,128)(2,1)S(1)}, u32[]{:S(2)}, u32[]{:S(2)}) collective-permute-start(bf16[384,768]{1,0:T(8,128)(2,1)S(1)} %select_convert_fusion.1), channel_id=1, source_target_pairs={{0,8},{4,12},{8,0},{12,4},{16,24},{20,28},{24,16},{28,20},{1,9},{5... | collective-permute-start | bytes 1769480 | tf_op jit(solution)/shard_map/ppermute | solution.py:366
  393.2 17.9 %collective-permute-start.20 = (bf16[96,768]{1,0:T(8,128)(2,1)}, bf16[96,768]{1,0:T(8,128)(2,1)}, u32[]{:S(2)}, u32[]{:S(2)}) collective-permute-start(bf16[96,768]{1,0:T(8,128)(2,1)} %select_convert_fusion.5), channel_id=1, source_target_pairs={{0,16},{4,20},{8,24},{12,28},{16,0},{20,4},{24,8},{28,12},{1,17},{... | collective-permute-start | bytes 442376 | tf_op jit(solution)/shard_map/ppermute | solution.py:366
  408.5 16.8 %collective-permute-start.31 = (bf16[192,768]{1,0:T(8,128)(2,1)}, bf16[192,768]{1,0:T(8,128)(2,1)}, u32[]{:S(2)}, u32[]{:S(2)}) collective-permute-start(bf16[192,768]{1,0:T(8,128)(2,1)} %select_convert_fusion.3), channel_id=1, source_target_pairs={{0,16},{4,20},{8,24},{12,28},{16,0},{20,4},{24,8},{28,12},{1,17},{... | collective-permute-start | bytes 884744 | tf_op jit(solution)/shard_map/ppermute | solution.py:366
  412.1 20.4 %collective-permute-start.21 = (bf16[96,768]{1,0:T(8,128)(2,1)S(1)}, bf16[96,768]{1,0:T(8,128)(2,1)S(1)}, u32[]{:S(2)}, u32[]{:S(2)}) collective-permute-start(bf16[96,768]{1,0:T(8,128)(2,1)S(1)} %add_convert_fusion.4), channel_id=1, source_target_pairs={{0,16},{4,20},{8,24},{12,28},{16,0},{20,4},{24,8},{28,12},{1,17},{... | collective-permute-start | bytes 442376 | tf_op jit(solution)/shard_map/ppermute | solution.py:366
  426.3 14.7 %collective-permute-start.32 = (bf16[192,768]{1,0:T(8,128)(2,1)S(1)}, bf16[192,768]{1,0:T(8,128)(2,1)S(1)}, u32[]{:S(2)}, u32[]{:S(2)}) collective-permute-start(bf16[192,768]{1,0:T(8,128)(2,1)S(1)} %add_convert_fusion.3), channel_id=1, source_target_pairs={{0,16},{4,20},{8,24},{12,28},{16,0},{20,4},{24,8},{28,12},{1,17},{... | collective-permute-start | bytes 884744 | tf_op jit(solution)/shard_map/ppermute | solution.py:366
  432.6 14.4 %collective-permute-start.22 = (bf16[192,768]{1,0:T(8,128)(2,1)S(1)}, bf16[192,768]{1,0:T(8,128)(2,1)S(1)}, u32[]{:S(2)}, u32[]{:S(2)}) collective-permute-start(bf16[192,768]{1,0:T(8,128)(2,1)S(1)} %pad_maximum_fusion.13), channel_id=1, source_target_pairs={{0,8},{4,12},{8,0},{12,4},{16,24},{20,28},{24,16},{28,20},{1,9},{5... | collective-permute-start | bytes 884744 | tf_op jit(solution)/shard_map/ppermute | solution.py:366
  441.1 17.8 %collective-permute-start.33 = (bf16[384,768]{1,0:T(8,128)(2,1)S(1)}, bf16[384,768]{1,0:T(8,128)(2,1)S(1)}, u32[]{:S(2)}, u32[]{:S(2)}) collective-permute-start(bf16[384,768]{1,0:T(8,128)(2,1)S(1)} %pad_maximum_fusion.6), channel_id=1, source_target_pairs={{0,8},{4,12},{8,0},{12,4},{16,24},{20,28},{24,16},{28,20},{1,9},{5... | collective-permute-start | bytes 1769480 | tf_op jit(solution)/shard_map/ppermute | solution.py:366
  447.1 19.6 %collective-permute-start.23 = (bf16[384,768]{1,0:T(8,128)(2,1)S(1)}, bf16[384,768]{1,0:T(8,128)(2,1)S(1)}, u32[]{:S(2)}, u32[]{:S(2)}) collective-permute-start(bf16[384,768]{1,0:T(8,128)(2,1)S(1)} %pad_maximum_fusion.5), channel_id=1, source_target_pairs={{0,4},{4,0},{8,12},{12,8},{16,20},{20,16},{24,28},{28,24},{1,5},{5... | collective-permute-start | bytes 1769480 | tf_op jit(solution)/shard_map/ppermute | solution.py:366
  459.3 27.4 %collective-permute-start.34 = (bf16[768,768]{1,0:T(8,128)(2,1)S(1)}, bf16[768,768]{1,0:T(8,128)(2,1)S(1)}, u32[]{:S(2)}, u32[]{:S(2)}) collective-permute-start(bf16[768,768]{1,0:T(8,128)(2,1)S(1)} %pad_maximum_fusion.2), channel_id=1, source_target_pairs={{0,4},{4,0},{8,12},{12,8},{16,20},{20,16},{24,28},{28,24},{1,5},{5... | collective-permute-start | bytes 3538952 | tf_op jit(solution)/shard_map/ppermute | solution.py:366
  (26 other events, 62.3 us)

commit v2 on v1

v2 whole, which is shorter than its diff:
```python
import functools
import math

import jax
import jax.numpy as jnp
from jax import lax
from jax.experimental import pallas as pl
from jax.experimental.pallas import tpu as pltpu
from jax.sharding import PartitionSpec as P

L = 128
HD = 64
EPS = 1e-05
F32 = jnp.float32
BF = jnp.bfloat16
NN = ((1,), (0,))
NT = ((1,), (1,))
TN = ((0,), (0,))
VMEM_LIMIT = 60 * 1024 * 1024
BIG = 64 * 1024


def dot(left, right, dims):
    return lax.dot_general(left, right, (dims, ((), ())), preferred_element_type=F32)


def exact(left, right, dims):
    return lax.dot_general(
        left, right, (dims, ((), ())), precision=lax.Precision.HIGHEST, preferred_element_type=F32
    )


class Loaded:
    def __init__(self, ref, copies=(), queue=None):
        self.ref, self.copies, self.queue = ref, list(copies), queue

    def __call__(self):
        if self.copies:
            while self.queue[0] and self not in self.queue[1]:
                advance(self.queue)
            for copy in self.copies:
                copy.wait()
            self.copies = []
            advance(self.queue)
        return self.ref


def advance(queue):
    if queue[0]:
        item = queue[0].pop(0)
        for copy in item.copies:
            copy.start()
        queue[1].append(item)


class Stored:
    def __init__(self, ref, copy=None):
        self.ref, self.copy, self.started = ref, copy, False

    def put(self):
        if self.copy is not None and not self.started:
            self.started = True
            self.copy.start()


def call(body, outs, args, flops, scratch=(), smem=(), place=None, window=4):
    place = place or {}
    size = lambda v: math.prod(v.shape) * v.dtype.itemsize
    moved = sum(size(v) for v in list(outs) + list(args))
    big_in = [i for i, v in enumerate(args) if i not in smem and size(v) >= BIG]
    held = [i for i in big_in if i not in place]
    big_out = [i for i, v in enumerate(outs) if size(v) >= BIG]
    n_in, n_out = len(args), len(outs)
    def kernel(*refs):
        ins = [Loaded(r) for r in refs[:n_in]]
        res = [Stored(r) for r in refs[n_in : n_in + n_out]]
        rest = refs[n_in + n_out :]
        held_in, rest = rest[: len(held)], rest[len(held) :]
        held_out, rest = rest[: len(big_out)], rest[len(big_out) :]
        extra, (sem_in, sem_out) = rest[:-2], rest[-2:]
        queue = ([], [])
        sem = 0
        for i in big_in:
            if i in place:
                dst, pairs = place[i](refs, extra)
            else:
                dst = held_in[held.index(i)]
                pairs = [(refs[i], dst)]
            copies = []
            for one, two in pairs:
                copies.append(pltpu.make_async_copy(one, two, sem_in.at[sem]))
                sem += 1
            ins[i] = Loaded(dst, copies, queue)
            queue[0].append(ins[i])
        for _ in range(window):
            advance(queue)
        for k, i in enumerate(big_out):
            copy = pltpu.make_async_copy(held_out[k], refs[n_in + i], sem_out.at[k])
            res[i] = Stored(held_out[k], copy)
        body(ins, res, extra)
        for item in ins:
            item()
        for item in res:
            item.put()
        for item in res:
            if item.copy is not None:
                item.copy.wait()

    def spec(i, big):
        if i in big:
            return pl.BlockSpec(memory_space=pl.ANY)
        return pl.BlockSpec(memory_space=pltpu.VMEM)

    return pl.pallas_call(
        kernel,
        out_shape=outs,
        in_specs=[
            pl.BlockSpec(memory_space=pltpu.SMEM) if i in smem else spec(i, big_in)
            for i in range(n_in)
        ],
        out_specs=[spec(i, big_out) for i in range(n_out)],
        scratch_shapes=[pltpu.VMEM(args[i].shape, args[i].dtype) for i in held]
        + [pltpu.VMEM(outs[i].shape, outs[i].dtype) for i in big_out]
        + list(scratch)
        + [pltpu.SemaphoreType.DMA((len(big_in) + 3 * len(place) + 1,)), pltpu.SemaphoreType.DMA((max(1, len(big_out)),))],
        cost_estimate=pl.CostEstimate(flops=int(flops), bytes_accessed=int(moved), transcendentals=0),
        compiler_params=pltpu.CompilerParams(vmem_limit_bytes=VMEM_LIMIT),
    )(*args)


def sds(shape, dtype):
    return jax.ShapeDtypeStruct(shape, dtype)


def head_mask(width):
    lane = lax.broadcasted_iota(jnp.int32, (1, width), 1)
    first = jnp.where(lane < width // 2, 1.0, 0.0)
    return first.astype(BF), (1.0 - first).astype(BF)


def doubled(pair, masks):
    return jnp.concatenate([pair * masks[0], pair * masks[1]], axis=0)


def far_places(j_at, first, scratch):
    def place_of(s, k):
        def pairs(refs, extra):
            dst = extra[scratch + s]
            n = dst.shape[0] // 4
            row = pl.multiple_of((refs[j_at][0] ^ k) * n, n)
            return dst, [(refs[first + 4 * s + k], dst.at[pl.ds(row, n), :])]

        return pairs

    return {first + 4 * s + k: place_of(s, k) for s in range(2) for k in range(4)}


class Whole:
    def __init__(self, parts):
        self.parts, self.ref = parts, parts[0].ref

    def __call__(self):
        for part in self.parts:
            part()
        return self.ref


class Rows:
    def __init__(self, item, lo, n):
        self.item, self.ref = item, item.ref.at[pl.ds(lo, n), :]

    def __call__(self):
        self.item()
        return self.ref


def side_by_side(a_ref, b_ref, row, w):
    a = a_ref[...].astype(F32)
    b = b_ref[...].astype(F32)
    return (a + pltpu.roll(b, w, 1))[row : row + 1, : 2 * w]


def joined(weights, w):
    return jnp.concatenate([q[k * w : (k + 1) * w, :] for k in range(3) for q in weights], axis=0)


def attn_fwd_core(x, weights, outs, biases, len_ref, qkv_ref, p_ref, mix_ref, stored):
    w = outs[0].ref.shape[0]
    rows = x.shape[0]
    seqs = rows // L
    wide = 2 * w
    total = dot(x, joined([q() for q in weights], w), NT)
    qkv_ref[:, :wide] = (total[:, :wide] + side_by_side(*biases, 0, w)).astype(BF)
    qkv_ref[:, wide : 2 * wide] = total[:, wide : 2 * wide].astype(BF)
    qkv_ref[:, 2 * wide :] = (total[:, 2 * wide :] + side_by_side(*biases, 1, w)).astype(BF)
    masks = head_mask(2 * HD)
    key_at = lax.broadcasted_iota(jnp.int32, (L, L), 0)
    pairs = wide // (2 * HD)

    def one(s, carry):
        at = pl.ds(pl.multiple_of(s * L, L), L)
        valid = key_at < len_ref[s]
        for pair in range(pairs):
            lo = pair * 2 * HD
            q = qkv_ref[at, lo : lo + 2 * HD]
            k = qkv_ref[at, wide + lo : wide + lo + 2 * HD]
            v = qkv_ref[at, 2 * wide + lo : 2 * wide + lo + 2 * HD]
            scores = dot(doubled(k, masks), q, NT) * HD ** (-0.5)
            lows = []
            for h in range(2):
                part = jnp.where(valid, scores[h * L : (h + 1) * L], -1e30)
                expo = jnp.exp(part - jnp.max(part, axis=0, keepdims=True))
                prob = expo * (1.0 / jnp.sum(expo, axis=0, keepdims=True))
                p_ref[s * pairs + pair, h * L : (h + 1) * L, :] = prob
                lows.append(prob.astype(BF))
            mixed = dot(jnp.concatenate(lows, axis=0), doubled(v, masks), TN)
            mix_ref[at, lo : lo + 2 * HD] = mixed.astype(BF)
        return carry

    lax.fori_loop(0, seqs, one, 0)
    stored()
    return dot(mix_ref[...], jnp.concatenate([o()[...] for o in outs], axis=0), NN)


def start_of(tok_ref, temb_ref):
    rows, width = tok_ref.shape
    seqs = rows // L
    return [
        tok_ref[s * L : (s + 1) * L, :].astype(F32) + temb_ref[s : s + 1, :] for s in range(seqs)
    ]


def attn_near_body(ins, res, extra):
    len_r, tok, temb, qa, qb, ba, bb, oa, ob = ins
    x, qkv, p, mix, acc = res
    for s, rows in enumerate(start_of(tok(), temb())):
        x.ref[s * L : (s + 1) * L, :] = rows.astype(BF)
    acc.ref[...] = attn_fwd_core(
        x.ref[...], (qa, qb), (oa, ob), (ba(), bb()), len_r(), qkv.ref, p.ref, mix.ref,
        lambda: [r.put() for r in (qkv, p, mix)],
    )


def far_weights(pieces):
    both = (Whole(pieces[:4]), Whole(pieces[4:]))
    w = both[0].ref.shape[0] // 4
    return both, tuple(Rows(f, 3 * w, w) for f in both)


def row_mean(value):
    return jnp.mean(value, axis=-1, keepdims=True)


def unit_of(value):
    centred = value - row_mean(value)
    rate = lax.rsqrt(row_mean(centred * centred) + EPS)
    return centred * rate, rate


def attn_far_body(ins, res, extra):
    len_r, j, x, *pieces, ba, bb, near, tok, temb, ob_v, g_v, s_v = ins
    qkv, p, mix, first_o, low = res
    weights, outs = far_weights(pieces)
    acc = attn_fwd_core(
        x()[...], weights, outs, (ba(), bb()), len_r(), qkv.ref, p.ref, mix.ref,
        lambda: [r.put() for r in (qkv, p, mix)],
    )
    out_bias, gain, shift = (vector(v) for v in (ob_v, g_v, s_v))
    first_ref = first_o.ref
    first_ref[...] = acc + near()[...] + out_bias
    for s, rows in enumerate(start_of(tok(), temb())):
        at = slice(s * L, (s + 1) * L)
        first = first_ref[at, :] + rows
        first_ref[at, :] = first
        unit, _ = unit_of(first)
        low.ref[at, :] = (unit * gain + shift).astype(BF)


def vector(item):
    return item()[...].astype(F32).reshape(1, -1)


def gelu_pair(pre):
    cdf = 0.5 * (1.0 + lax.erf(pre * 0.7071067811865476))
    pdf = jnp.exp(-0.5 * pre * pre) * 0.3989422804014327
    return pre * cdf, cdf + pre * pdf


def mlp_fwd_core(x_ref, ups, downs, biases, act_ref, slope_ref, acc_ref, done):
    rows = x_ref.shape[0]
    hid = ups[0].ref.shape[0]
    tile = 384 if hid % 384 == 0 else hid
    block = 256 if rows % 256 == 0 else rows
    first = True
    for r in range(len(ups)):
        for t in range(hid // tile):
            up = ups[r]()[t * tile : (t + 1) * tile, :]
            down = downs[r]()[t * tile : (t + 1) * tile, :]
            bias = biases[r][:, t * tile : (t + 1) * tile].astype(F32)
            for m in range(rows // block):
                at = slice(m * block, (m + 1) * block)
                act, slope = gelu_pair(dot(x_ref[at, :], up, NT) + bias)
                low = act.astype(BF)
                cols = slice(t * tile, (t + 1) * tile)
                act_ref[r][at, cols] = low
                slope_ref[r][at, cols] = slope
                part = dot(low, down, NN)
                if first:
                    acc_ref[at, :] = part
                else:
                    acc_ref[at, :] += part
            first = False
        done(r)


def mlp_near_body(ins, res, extra):
    x, ua, ub, da, db, ba, bb = ins
    act_a, act_b, slope_a, slope_b, acc = res

    def done(r):
        (act_a, act_b)[r].put()
        (slope_a, slope_b)[r].put()

    mlp_fwd_core(
        x(), (ua, ub), (da, db), (ba()[2:3, :], bb()[2:3, :]), (act_a.ref, act_b.ref),
        (slope_a.ref, slope_b.ref), acc.ref, done,
    )


def mlp_far_body(ins, res, extra):
    j, x, *pieces, ba, bb, near, first, cot, g1_v, s1_v, b_v, g2_v, s2_v = ins
    fa, fb = Whole(pieces[:4]), Whole(pieces[4:])
    dub, ddb, dua, dda, bsb, bsa, out, grad, sums, gn = res
    _, _, act_a, act_b, slope_a, slope_b, acc_ref = extra
    hid = fa.ref.shape[0] // 2
    ups = tuple(Rows(f, 0, hid) for f in (fa, fb))
    downs = tuple(Rows(f, hid, hid) for f in (fa, fb))
    mlp_fwd_core(
        x(), ups, downs, (ba()[2:3, :], bb()[2:3, :]), (act_a, act_b), (slope_a, slope_b), acc_ref,
        lambda r: None,
    )
    rows, width = x().shape
    first_ref, near_ref, cot_ref, sums_ref = first(), near(), cot(), sums.ref
    gain1, shift1, bias, gain, shift = [vector(v) for v in (g1_v, s1_v, b_v, g2_v, s2_v)]
    sums_ref[...] = jnp.zeros_like(sums_ref)
    for s in range(rows // L):
        at = slice(s * L, (s + 1) * L)
        unit1, _ = unit_of(first_ref[at, :])
        normed = unit1 * gain1 + shift1
        second = normed + acc_ref[at, :] + near_ref[at, :] + bias
        unit, rate = unit_of(second)
        out.ref[at, :] = (unit * gain + shift).astype(BF)
        grad_out = cot_ref[at, :].astype(F32)
        inner = grad_out * gain
        lower = rate * (inner - row_mean(inner) - unit * row_mean(inner * unit))
        grad.ref[at, :] = lower
        sums_ref[0:1, :] += jnp.sum(grad_out * unit, axis=0, keepdims=True)
        sums_ref[1:2, :] += jnp.sum(grad_out, axis=0, keepdims=True)
        sums_ref[2:3, :] += jnp.sum(lower, axis=0, keepdims=True)
    out.put()
    gl = grad.ref[...].astype(BF)
    held = [Loaded(r) for r in (act_a, act_b, slope_a, slope_b)]
    gn.ref[...] = mlp_bwd_slice(x, gl, ups[1], downs[1], held[1], held[3], dub, ddb, bsb)
    gn.ref[...] += mlp_bwd_slice(x, gl, ups[0], downs[0], held[0], held[2], dua, dda, bsa)


def mlp_bwd_slice(x, gl, up, down, act, slope, du, dd, bsum):
    dd.ref[...] = dot(act()[...], gl, TN).astype(dd.ref.dtype)
    dd.put()
    gp = (dot(gl, down()[...], NT) * slope()[...]).astype(BF)
    bsum.ref[...] = jnp.sum(gp.astype(F32), axis=0, keepdims=True)
    du.ref[...] = dot(gp, x()[...], TN).astype(du.ref.dtype)
    du.put()
    return dot(gp, up()[...], NN)


def mlp_bwd_near_body(ins, res, extra):
    g, act_b, db, slope_b, x, ub, act_a, da, slope_a, ua, far, first, g_v = ins
    dub, ddb, dua, dda, bsb, bsa, gf, sums = res
    gl = g()[...].astype(BF)
    gf_ref, sums_ref = gf.ref, sums.ref
    gf_ref[...] = mlp_bwd_slice(x, gl, ub, db, act_b, slope_b, dub, ddb, bsb)
    gf_ref[...] += mlp_bwd_slice(x, gl, ua, da, act_a, slope_a, dua, dda, bsa)
    rows = x().shape[0]
    far_ref, first_ref, g_ref = far(), first(), g()
    gain = vector(g_v)
    sums_ref[...] = jnp.zeros_like(sums_ref)
    for s in range(rows // L):
        at = slice(s * L, (s + 1) * L)
        unit, rate = unit_of(first_ref[at, :])
        upper = gf_ref[at, :] + far_ref[at, :] + g_ref[at, :]
        inner = upper * gain
        lower = rate * (inner - row_mean(inner) - unit * row_mean(inner * unit))
        gf_ref[at, :] = lower
        sums_ref[0:1, :] += jnp.sum(upper * unit, axis=0, keepdims=True)
        sums_ref[1:2, :] += jnp.sum(upper, axis=0, keepdims=True)
        sums_ref[2:3, :] += jnp.sum(lower, axis=0, keepdims=True)


def attn_bwd_core(x, gl, weights, outs, qkv, p, mix, da, db, bsum_ref, gm_ref, dj_ref):
    rows = gl.shape[0]
    seqs = rows // L
    w = outs[0].ref.shape[0]
    wide = 2 * w
    gm_ref[...] = dot(gl, jnp.concatenate([o()[...] for o in outs], axis=0), NT).astype(BF)
    dout = dot(mix()[...], gl, TN)
    da.ref[3 * w : 4 * w, :] = dout[:w].astype(da.ref.dtype)
    db.ref[3 * w : 4 * w, :] = dout[w:].astype(db.ref.dtype)
    masks = head_mask(2 * HD)
    half = lax.broadcasted_iota(jnp.int32, (L, 2 * HD), 1) < HD
    pairs = wide // (2 * HD)
    scale = HD ** (-0.5)
    qkv_ref, p_ref = qkv(), p()

    def one(s, carry):
        at = pl.ds(pl.multiple_of(s * L, L), L)
        for pair in range(pairs):
            lo = pair * 2 * HD
            q = qkv_ref[at, lo : lo + 2 * HD]
            k = qkv_ref[at, wide + lo : wide + lo + 2 * HD]
            v = qkv_ref[at, 2 * wide + lo : 2 * wide + lo + 2 * HD]
            go = gm_ref[at, lo : lo + 2 * HD]
            prob = p_ref[s * pairs + pair]
            dv = dot(prob.astype(BF), go, NN)
            dp = dot(doubled(v, masks), go, NT)
            lows = []
            for h in range(2):
                ph = prob[h * L : (h + 1) * L]
                dh = dp[h * L : (h + 1) * L]
                delta = jnp.sum(ph * dh, axis=0, keepdims=True)
                lows.append((ph * (dh - delta)).astype(BF))
            ds = jnp.concatenate(lows, axis=0)
            dk = dot(ds, q, NN)
            dq = dot(ds, doubled(k, masks), TN) * scale
            dj_ref[at, lo : lo + 2 * HD] = dq.astype(BF)
            dj_ref[at, wide + lo : wide + lo + 2 * HD] = (
                jnp.where(half, dk[:L], dk[L:]) * scale
            ).astype(BF)
            dj_ref[at, 2 * wide + lo : 2 * wide + lo + 2 * HD] = jnp.where(
                half, dv[:L], dv[L:]
            ).astype(BF)
        return carry

    lax.fori_loop(0, seqs, one, 0)
    dj = dj_ref[...]
    grads = dot(dj, x()[...], TN)
    for k in range(3):
        lo = k * wide
        da.ref[k * w : (k + 1) * w, :] = grads[lo : lo + w].astype(da.ref.dtype)
        db.ref[k * w : (k + 1) * w, :] = grads[lo + w : lo + wide].astype(db.ref.dtype)
    db.put()
    da.put()
    bsum_ref[...] = jnp.zeros_like(bsum_ref)
    bsum_ref[0:1, :] = jnp.sum(dj[:, :wide].astype(F32), axis=0, keepdims=True)
    bsum_ref[1:2, :] = jnp.sum(dj[:, 2 * wide :].astype(F32), axis=0, keepdims=True)
    return dot(dj, joined([q() for q in weights], w), NN)


def attn_bwd_far_body(ins, res, extra):
    j, g, *pieces, mix, qkv, p, x = ins
    db, da, bsum, acc = res
    _, _, gm_ref, dj_ref = extra
    weights, outs = far_weights(pieces)
    gl = g()[...].astype(BF)
    acc.ref[...] = attn_bwd_core(
        x, gl, weights, outs, qkv, p, mix, da, db, bsum.ref, gm_ref, dj_ref
    )


def attn_bwd_near_body(ins, res, extra):
    t, g, oa, ob, mix, qkv, p, x, qa, qb, far, sums2, sums1, b0, b1, b2, b3, far_bsum, steps = ins
    db, da, gt, pack = res
    gm_ref, dj_ref, bsum_ref = extra
    bsum = Loaded(bsum_ref)
    gl = g()[...].astype(BF)
    gt.ref[...] = (
        attn_bwd_core(
            x, gl, (qa, qb), (oa, ob), qkv, p, mix, da, db, bsum.ref, gm_ref, dj_ref
        )
        + far()[...]
        + g()[...]
    )
    gt.put()
    pack_ref = pack.ref
    pack_ref[...] = jnp.zeros_like(pack_ref)
    pack_ref[0:3, :] = sums2()[0:3, :]
    pack_ref[3:6, :] = sums1()[0:3, :]
    wide = far_bsum.ref.shape[1]
    for r, bias in enumerate((b0, b1, b2, b3)):
        at = t()[0] ^ r
        pack_ref[pl.ds(8 + at, 1), :] = bias()[...]
        sums = (bsum_ref if r < 2 else far_bsum())[...]
        if r % 2:
            sums = pltpu.roll(sums, wide - wide // 2, 1)
        for k in range(2):
            pack_ref[pl.ds(12 + 4 * k + at, 1), :wide] = sums[k : k + 1, :]
    for s in range(gl.shape[0] // L):
        pack_ref[24 + s : 25 + s, :] = jnp.sum(gt.ref[s * L : (s + 1) * L, :], axis=0, keepdims=True)
    pack_ref[31:32, :] = steps()[...]


def halves_at(bit, n):
    keep = pl.multiple_of(bit * n, n)
    send = pl.multiple_of((1 - bit) * n, n)
    return pl.ds(keep, n), pl.ds(send, n)


def cut(refs, bit, keep, send, scale=1):
    n = keep.ref.shape[0]
    for at, out in zip(halves_at(bit, n), (keep, send)):
        total = refs[0][at, :].astype(F32)
        for ref in refs[1:]:
            total = total + ref[at, :].astype(F32)
        out.ref[...] = total.astype(out.ref.dtype)


def pair_sum(one, two, at, out):
    out.ref[...] = (one[at, :].astype(F32) + two[at, :].astype(F32)).astype(out.ref.dtype)


def glue_first_body(ins, res, extra):
    bits, dd, dd2, du, du2 = ins
    d_keep, d_send, u_keep, u_send = res
    cut((dd(), dd2()), bits()[0], d_keep, d_send)
    d_send.put()
    cut((du(), du2()), bits()[1], u_keep, u_send)


def glue_second_body(ins, res, extra):
    bits, dn, dn2, un, un2, df, df_x, uf, uf_z = ins
    dn_keep, un_keep, df_keep, uf_keep, x_send, z_send = res
    n = dn_keep.ref.shape[0]
    first = lambda out: Stored(out.ref.at[pl.ds(0, n), :])
    rest = lambda out: Stored(out.ref.at[pl.ds(n, n // 2), :])
    cut((dn(), dn2()), bits()[0], dn_keep, first(x_send))
    cut((un(), un2()), bits()[1], un_keep, first(z_send))
    cut((df(), df_x()), bits()[1], df_keep, rest(z_send))
    cut((uf(), uf_z()), bits()[0], uf_keep, rest(x_send))


def glue_third_body(ins, res, extra):
    bits, da, da2, dn, un, df, uf, x_got, z_got = ins
    a_lo, a_hi, dn_keep, dn_send, un_keep, un_send, df_keep, uf_keep, f_send = res
    n = a_lo.ref.shape[0]
    pair_sum(da(), da2(), slice(0, n), a_lo)
    a_lo.put()
    pair_sum(da(), da2(), slice(n, 2 * n), a_hi)
    a_hi.put()
    n = dn.ref.shape[0]
    first = lambda item: item().at[pl.ds(0, n), :]
    rest = lambda item: item().at[pl.ds(n, n // 2), :]
    cut((dn(), first(x_got)), bits()[1], dn_keep, dn_send)
    cut((un(), first(z_got)), bits()[0], un_keep, un_send)
    k = df_keep.ref.shape[0]
    part = lambda i: Stored(f_send.ref.at[pl.ds(i * k, k), :])
    cut((df(), rest(z_got)), bits()[2], df_keep, part(0))
    cut((uf(), rest(x_got)), bits()[2], uf_keep, part(1))


def glue_fourth_body(ins, res, extra):
    bits, dn, dn_z, un, un_x, df, uf, f_got = ins
    keep, send, f_sum = res
    n = df.ref.shape[0]
    part = lambda out, i: Stored(out.ref.at[pl.ds(i * n, n), :])
    cut((dn(), dn_z()), bits()[2], part(keep, 0), part(send, 0))
    cut((un(), un_x()), bits()[2], part(keep, 1), part(send, 1))
    got = f_got()
    for i, item in enumerate((df, uf)):
        rows = slice(i * n, (i + 1) * n)
        f_sum.ref[rows, :] = (item()[...] + got[rows, :].astype(F32)).astype(f_sum.ref.dtype)


def quarter_of(bits, m):
    return (bits[0] ^ (m & 1)) * 2 + (bits[1] ^ (m >> 1))


def glue_fifth_body(ins, res, extra):
    bits, da, da2, lo, hi = ins
    n = res[0].ref.shape[0]
    a, b, lo_ref, hi_ref = da(), da2(), lo(), hi()
    for m in (1, 2, 3, 0):
        out = res[m]
        at = quarter_of(bits(), m)
        rows = pl.ds(pl.multiple_of(at * n, n), n)
        part = pl.ds(pl.multiple_of((at & 1) * n, n), n)
        total = a[rows, :] + b[rows, :].astype(F32)

        @pl.when(at < 2)
        def _():
            out.ref[...] = (total + lo_ref[part, :].astype(F32)).astype(out.ref.dtype)

        @pl.when(at >= 2)
        def _():
            out.ref[...] = (total + hi_ref[part, :].astype(F32)).astype(out.ref.dtype)

        out.put()


def join_body(ins, res, extra):
    bits, d_own, d_x, u_own, u_z, *quarters = ins
    d_out, u_out, q_out, o_out = res
    n = d_own.ref.shape[0]
    for own, other, out, bit in ((d_own, d_x, d_out, 0), (u_own, u_z, u_out, 1)):
        for item, at in zip((own, other), halves_at(bits()[bit], n)):
            out.ref[at, :] = item()[...].astype(F32)
        out.put()
    n = quarters[0].ref.shape[0]
    for m, item in enumerate(quarters):
        at = quarter_of(bits(), m)
        value = item()[...].astype(F32)

        @pl.when(at < 3)
        def _():
            q_out.ref[pl.ds(pl.multiple_of(at * n, n), n), :] = value

        @pl.when(at == 3)
        def _():
            o_out.ref[...] = value


def last_body(ins, res, extra):
    t, feats, inner, ibias, outer, grad, small = ins
    g_inner, g_ibias, g_outer, g_obias, *vectors, own_bup, own_q, own_v = res
    outer_w = outer()[...].astype(F32)
    pre = exact(feats()[...], inner()[...].astype(F32), NN) + vector(ibias)
    gate = 1.0 / (1.0 + jnp.exp(-pre))
    g = grad()[...]
    g_outer.ref[...] = exact(pre * gate, g, TN)
    g_outer.put()
    g_obias.ref[...] = jnp.sum(g, axis=0)
    hidden = exact(g, outer_w, NT) * (gate * (1.0 + pre * (1.0 - gate)))
    g_inner.ref[...] = exact(feats()[...], hidden, TN)
    g_ibias.ref[...] = jnp.sum(hidden, axis=0)
    small_ref = small()
    for i, out in enumerate(vectors):
        out.ref[...] = small_ref[i, :]
    own_bup.ref[...] = small_ref[pl.ds(8 + t()[0], 1), :].reshape(own_bup.ref.shape)
    for k, out in enumerate((own_q, own_v)):
        out.ref[...] = small_ref[pl.ds(12 + 4 * k + t()[0], 1), :]


def time_features(timesteps, width):
    half = width // 2
    frequency = jnp.exp(-math.log(10000.0) * jnp.arange(half, dtype=F32) / half)
    angles = timesteps.astype(F32)[:, None] * frequency[None, :]
    return jnp.concatenate([jnp.cos(angles), jnp.sin(angles)], axis=1)


def swap(value, axis, size, bit):
    return lax.ppermute(value, axis, [(i, i ^ bit) for i in range(size)])


def tie(value, *others):
    return lax.optimization_barrier((value,) + others)[0]


def halves(bit_set, mine, other):
    low = jnp.where(bit_set, other, mine)
    high = jnp.where(bit_set, mine, other)
    return low, high


def tie(value, *others):
    return lax.optimization_barrier((value,) + others)[0]


def sync(*values):
    return lax.optimization_barrier(values)


def local(dp, tensor, *args):
    (
        tokens, timesteps, lengths, time_inner, time_ibias, time_outer, time_obias, qkv_weight,
        qv_bias, out_weight, out_bias, gain_first, shift_first, up_weight, up_bias, down_weight,
        down_bias, gain_second, shift_second, cotangent,
    ) = args
    rows, width = tokens.shape
    seqs = rows // L
    w = qkv_weight.shape[2]
    hid = up_weight.shape[0]
    t = lax.axis_index("tensor")
    d = lax.axis_index("dp")
    high = list(range(3, dp.bit_length() - 1))
    core = lambda v: swap(v, "tensor", tensor, 1)
    across = lambda v: swap(v, "tensor", tensor, 2)

    j0 = (d & 1) == 1
    j1 = ((d >> 1) & 1) == 1
    own_j = (d & 3)[None]
    own_bits = jnp.stack([d & 1, (d >> 1) & 1, (d >> 2) & 1])
    flat_qkv = jnp.transpose(qkv_weight, (1, 2, 0)).reshape(3 * w, width)
    part_a = [flat_qkv[:w], flat_qkv[w : 2 * w], flat_qkv[2 * w :], out_weight]
    h2 = hid // 2
    part_f = [up_weight[:h2], up_weight[h2:], down_weight[:h2], down_weight[h2:]]

    def pick(parts, j0, j1):
        return jnp.where(j1, jnp.where(j0, parts[3], parts[2]), jnp.where(j0, parts[1], parts[0]))

    def spread(got):
        return [swap(got, "dp", dp, m) for m in (1, 2)]

    a_y = across(pick(part_a, j0, j1))
    qkv_core, out_core = core(flat_qkv), core(out_weight)
    bias = jnp.concatenate(
        [
            jnp.pad(qv_bias, ((0, 0), (0, width - w))),
            jnp.pad(up_bias[None], ((0, 13), (0, 0))),
        ],
        axis=0,
    )
    bias_core, bias_y = core(bias), across(bias)

    features = time_features(timesteps, time_inner.shape[0])
    hidden_time = jax.nn.silu(
        exact(features, time_inner.astype(F32), NN) + time_ibias.astype(F32)
    )
    temb = exact(hidden_time, time_outer.astype(F32), NN) + time_obias.astype(F32)
    temb = jnp.pad(temb, ((0, 8 - seqs), (0, 0))) if seqs < 8 else temb
    own_len = lax.dynamic_slice(lengths, (t * seqs,), (seqs,))

    send_a, send_f, a_y, temb = sync(
        pick(part_a, ~j0, ~j1), pick(part_f, j0, j1), a_y, temb
    )
    a_others = spread(a_y)
    a_others.append(across(send_a))
    f_y = across(send_f)
    wide = 2 * w
    pairs = wide // (2 * HD)
    act_shapes = [
        sds((rows, 3 * wide), BF),
        sds((seqs * pairs, 2 * L, L), F32),
        sds((rows, wide), BF),
    ]
    full = sds((rows, width), F32)
    low_full = sds((rows, width), BF)
    attn_flops = 2 * rows * width * 4 * wide + 4 * rows * L * wide
    x, qkv_n, p_n, mix_n, acc_n = call(
        attn_near_body, [low_full] + act_shapes + [full],
        (own_len, tokens, temb, flat_qkv, qkv_core, bias, bias_core, out_weight, out_core),
        attn_flops, smem=(0,),
    )
    acc_n, bias_y, f_y, *far_a1 = sync(acc_n, bias_y, f_y, a_y, *a_others)
    far_a2 = [core(v) for v in far_a1]
    bias_y2 = core(bias_y)
    f_others = spread(f_y)
    f_others.append(across(tie(pick(part_f, ~j0, ~j1), f_y)))
    up_core, down_core = core(up_weight), core(down_weight)
    wt = pltpu.VMEM((4 * w, width), BF)
    qkv_f, p_f, mix_f, first, normed = call(
        attn_far_body, act_shapes + [full, low_full],
        (
            own_len, own_j, x, *far_a1, *far_a2, bias_y, bias_y2, acc_n,
            tokens, temb, out_bias, gain_first, shift_first,
        ),
        attn_flops, smem=(0, 1), scratch=[wt, wt], place=far_places(1, 3, 0),
    )
    normed, up_core, down_core, *far_f1 = sync(normed, up_core, down_core, f_y, *f_others)
    far_f2 = [core(v) for v in far_f1]
    up_core, down_core = up_core, down_core
    mlp_flops = 2 * rows * width * 4 * hid
    act_na, act_nb, slope_na, slope_nb, mlp_n = call(
        mlp_near_body,
        [sds((rows, hid), BF)] * 2 + [sds((rows, hid), F32)] * 2 + [full],
        (normed, up_weight, up_core, down_weight, down_core, bias, bias_core), mlp_flops,
    )
    mlp_n, *far_f2 = sync(mlp_n, *far_f2)
    mat = pltpu.VMEM((2 * hid, width), BF)
    dw_far = sds((hid, width), BF)
    dw_own = sds((hid, width), F32)
    bsum = sds((1, hid), F32)
    dws = [dw_far, dw_far, dw_own, dw_own, bsum, bsum]
    sums_shape = sds((8, width), F32)
    duf2, ddf2, duf, ddf, bup_f2, bup_f, layer_out, g2, sums2, gn_f = call(
        mlp_far_body, dws + [low_full, full, sums_shape, full],
        (
            own_j, normed, *far_f1, *far_f2, bias_y, bias_y2, mlp_n,
            first, cotangent, gain_first, shift_first, down_bias, gain_second, shift_second,
        ),
        3 * mlp_flops, smem=(0,),
        scratch=[
            mat, mat, pltpu.VMEM((rows, hid), BF), pltpu.VMEM((rows, hid), BF),
            pltpu.VMEM((rows, hid), F32), pltpu.VMEM((rows, hid), F32),
            pltpu.VMEM((rows, width), F32),
        ],
        place=far_places(0, 2, 0),
    )
    f32 = lambda v: v.astype(F32)

    part = lambda k, dtype: sds((hid // k, width), dtype)

    def glue(body, outs, args):
        return call(body, outs, (own_bits,) + args, 1, smem=(0,), window=16)

    df_keep, df_send, uf_keep, uf_send = glue(
        glue_first_body, [part(2, F32), part(2, BF), part(2, F32), part(2, BF)],
        (ddf, core(ddf2), duf, core(duf2)),
    )
    g2n, df_keep, df_send, uf_keep, uf_send = sync(g2, df_keep, df_send, uf_keep, uf_send)
    along = lambda v, m: swap(v, "dp", dp, m)
    df_x = along(df_send, 1)
    uf_z = along(uf_send, 2)
    dun2, ddn2, dun, ddn, bup_n2, bup_n, g1, sums1 = call(
        mlp_bwd_near_body, dws + [full, sums_shape],
        (
            g2n, act_nb, down_core, slope_nb, normed, up_core, act_na, down_weight, slope_na,
            up_weight, gn_f, first, gain_first,
        ),
        2 * mlp_flops,
    )
    dun2, ddn2, g1, df_x, uf_z = sync(dun2, ddn2, g1, df_x, uf_z)
    both = sds((hid // 2 + hid // 4, width), BF)
    dn_keep, un_keep, df_keep, uf_keep, x_send, z_send = glue(
        glue_second_body, [part(2, F32), part(2, F32), part(4, F32), part(4, F32), both, both],
        (ddn, core(ddn2), dun, core(dun2), df_keep, df_x, uf_keep, uf_z),
    )
    g1, dn_keep, un_keep, df_keep, uf_keep, x_send, z_send = sync(
        g1, dn_keep, un_keep, df_keep, uf_keep, x_send, z_send
    )
    x_got = along(x_send, 1)
    z_got = along(z_send, 2)
    da_shapes = [sds((4 * w, width), BF), sds((4 * w, width), F32), sds((8, wide), F32)]
    bwd_scratch = [pltpu.VMEM((rows, wide), BF), pltpu.VMEM((rows, 3 * wide), BF)]
    daf2, daf, qvb_f, gin_f = call(
        attn_bwd_far_body, da_shapes + [full],
        (own_j, g1, *far_a1, *far_a2, mix_f, qkv_f, p_f, x), 2 * attn_flops,
        smem=(0,), scratch=[wt, wt] + bwd_scratch, place=far_places(0, 2, 0),
    )
    daf2, gin_f, x_got, z_got = sync(daf2, gin_f, x_got, z_got)
    qpart = lambda k, dtype: sds((4 * w // k, width), dtype)
    a_lo, a_hi, dn_keep, dn_send, un_keep, un_send, df_keep, uf_keep, f_send = glue(
        glue_third_body,
        [
            qpart(2, BF), qpart(2, BF), part(4, F32), part(4, BF), part(4, F32), part(4, BF),
            part(8, F32), part(8, F32), part(4, BF),
        ],
        (daf, core(daf2), dn_keep, un_keep, df_keep, uf_keep, x_got, z_got),
    )
    g1, a_lo, a_hi, dn_keep, dn_send, un_keep, un_send, df_keep, uf_keep, f_send = sync(
        g1, a_lo, a_hi, dn_keep, dn_send, un_keep, un_send, df_keep, uf_keep, f_send
    )
    a_lo = across(a_lo)
    dn_z = along(dn_send, 2)
    un_x = along(un_send, 1)
    f_got = along(f_send, 4)
    steps_row = jnp.pad(timesteps.astype(F32), (0, width - seqs))[None, :]
    dan2, dan, grad_tokens, pack = call(
        attn_bwd_near_body, da_shapes[:2] + [full, sds((32, width), F32)],
        (
            t[None], g1, out_weight, out_core, mix_n, qkv_n, p_n, x, flat_qkv, qkv_core, gin_f,
            sums2, sums1, bup_n, bup_n2, bup_f, bup_f2, qvb_f, steps_row,
        ),
        2 * attn_flops, smem=(0,), scratch=bwd_scratch + [pltpu.VMEM((8, wide), F32)],
    )
    dan2, pack, a_hi, a_lo, dn_z, un_x, f_got = sync(dan2, pack, a_hi, a_lo, dn_z, un_x, f_got)

    cat = lambda *v: jnp.concatenate(v, axis=0)
    near_a2, pack_c = core(dan2), core(pack)
    a_hi = across(a_hi)
    du_keep, du_send, f_sum = glue(
        glue_fourth_body, [part(4, F32), part(4, BF), part(4, BF if not high else F32)],
        (dn_keep, dn_z, un_keep, un_x, df_keep, uf_keep, f_got),
    )

    def halve(value, which):
        n = value.shape[0] // 2
        at = jnp.where(((d >> which) & 1) == 1, n, 0)
        keep = lax.dynamic_slice_in_dim(value, at, n, 0)
        return keep, lax.dynamic_slice_in_dim(value, n - at, n, 0).astype(BF)

    def high_sum(value):
        for which in high:
            keep, send = halve(value, which)
            value = keep + f32(along(send, 1 << which))
        return value

    def join_bit(value, which, other=None):
        other = along(value, 1 << which) if other is None else other
        return cat(*halves(((d >> which) & 1) == 1, value, other))

    def high_join(value):
        for which in high[::-1]:
            value = join_bit(value, which)
        return value

    two = lambda f, v: cat(f(v[: v.shape[0] // 2]), f(v[v.shape[0] // 2 :]))
    du_z = along(du_send, 4)
    du_y = across(two(high_sum, f_sum).astype(BF) if high else f_sum)
    near_a2, pack_c, a_hi, du_z, du_y = sync(near_a2, pack_c, a_hi, du_z, du_y)

    du = two(high_sum, du_keep + f32(du_z)) + f32(du_y)
    du = two(high_join, du.astype(BF))
    small = pack[:24] + pack_c[:24]
    gath = cat(*halves((t & 1) == 1, pack[24:], pack_c[24:]))
    got_y = across(cat(small, gath))
    du_z = along(du, 4)
    quarters = glue(
        glue_fifth_body, [qpart(4, F32)] + [qpart(4, BF)] * 3, (dan, near_a2, a_lo, a_hi)
    )
    got = [along(quarters[m], m) for m in (1, 2, 3)]
    got_y, du, du_z, *got = sync(got_y, du, du_z, *got)

    state = [small + got_y[:24], cat(*halves((t & 2) == 2, gath, got_y[24:]))]

    def small_hop(which):
        small, gath = state
        other = along(cat(small, gath), 1 << which)
        state[:] = [small + other[:24], join_bit(gath, which, other[24:])]

    a_keep, a_send = halve(quarters[0] + sum(f32(v) for v in got), 2)
    a_z = along(a_send, 4)
    n = du.shape[0] // 2
    d_own, u_own = join_bit(du[:n], 2, du_z[:n]), join_bit(du[n:], 2, du_z[n:])
    d_z, u_x = along(d_own, 2), along(u_own, 1)
    small_hop(0)
    a_keep, a_z, d_own, u_own, d_z, u_x, *state[:] = sync(
        a_keep, a_z, d_own, u_own, d_z, u_x, *state
    )
    a_end = high_join(high_sum(a_keep + f32(a_z)).astype(BF))
    a_z = along(a_end, 4)
    d_own, u_own = join_bit(d_own, 1, d_z), join_bit(u_own, 0, u_x)
    d_x, u_z = along(d_own, 1), along(u_own, 2)
    small_hop(1)
    a_end, a_z, d_own, u_own, d_x, u_z, *state[:] = sync(
        a_end, a_z, d_own, u_own, d_x, u_z, *state
    )
    a_end = join_bit(a_end, 2, a_z)
    a_got = [along(a_end, m) for m in (1, 2, 3)]
    small_hop(2)
    for which in high:
        small_hop(which)

    small, gath = state
    gath = gath.reshape(dp, tensor, 8, width)
    feats = time_features(gath[:, :, 7, :seqs].reshape(-1), time_inner.shape[0])
    line = sds((width,), F32)
    row = sds((1, width), F32)
    (
        grad_tinner, grad_tibias, grad_touter, grad_tobias, gsecond, ssecond, bdown, gfirst, sfirst,
        bout, own_bup, own_q, own_v,
    ) = call(
        last_body,
        [sds(time_inner.shape, F32), sds(time_ibias.shape, F32), sds(time_outer.shape, F32)]
        + [line] * 8 + [row] * 2,
        (
            t[None], feats, time_inner, time_ibias, time_outer,
            gath[:, :, :seqs].reshape(-1, width), small,
        ),
        1, smem=(0,), window=8,
    )
    d_all, u_all, q_all, o_all = call(
        join_body, [part(1, F32)] * 2 + [sds((3 * w, width), F32), sds((w, width), F32)],
        (own_bits, d_own, d_x, u_own, u_z, a_end, *a_got), 1, smem=(0,), window=16,
    )

    grad_qkv = jnp.transpose(q_all.reshape(3, w, width), (2, 0, 1))
    return (
        layer_out,
        grad_tokens,
        grad_tinner,
        grad_tibias,
        grad_touter,
        grad_tobias,
        grad_qkv,
        jnp.concatenate([own_q[:, :w], own_v[:, :w]], axis=0),
        o_all,
        bout,
        gfirst,
        sfirst,
        u_all,
        own_bup,
        d_all,
        bdown,
        gsecond,
        ssecond,
    )


def solution(mesh):
    both = ("dp", "tensor")
    placed = (
        P(both, None), P(both), P("dp"), P(), P(), P(), P(), P(None, None, "tensor"),
        P(None, "tensor"), P("tensor", None), P(), P(), P(), P("tensor", None), P("tensor"),
        P("tensor", None), P(), P(), P(), P(both, None),
    )
    return jax.shard_map(
        functools.partial(local, mesh.shape["dp"], mesh.shape["tensor"]),
        mesh=mesh,
        in_specs=placed,
        out_specs=(
            P(both, None), P(both, None), P(), P(), P(), P(), P(None, None, "tensor"),
            P(None, "tensor"), P("tensor", None), P(), P(), P(), P("tensor", None), P("tensor"),
            P("tensor", None), P(), P(), P(),
        ),
        check_vma=False,
    )
```

time: 497 us -> 336 us (0.68)
  waiting for transfers between devices: 237 us -> 97.2 us
  blocking collectives: 40.7 us -> 0 us
  Pallas kernels: 117 us -> 153 us
  starting transfers between devices: 30.9 us -> 54.6 us
  other arithmetic: 29.9 us -> 10.8 us
  local copies, waits for them, and re-layouts: 27.2 us -> 11 us
  matrix products: 6.43 us -> 0.65 us
    ppermute x35 -> x58, waiting for transfers between devices: 237 us -> 97.2 us  [swap(): return lax.ppermute(value, axis, [(i, i ^ bit) for i in range(size)])]
    unnamed x1 -> x0, blocking collectives: 40.7 us -> none
    pallas_call x8 -> x14, Pallas kernels: 117 us -> 153 us  [call(): pl.pallas_call(kernel, out_shape=outs, in_specs=[pl.BlockSpec(memory_spac...]
    ppermute x35 -> x58, starting transfers between devices: 30.9 us -> 54.6 us  [swap(): return lax.ppermute(value, axis, [(i, i ^ bit) for i in range(size)])]
    slice x16 -> x3, local copies, waits for them, and re-layouts: 14.2 us -> 1.42 us  [the longest x1 0.69 us: local(): own_q[:, :w]]
    dot_general x6 -> x2, matrix products: 6.43 us -> 0.65 us  [exact(): lax.dot_general(left, right, (dims, ((), ())), precision=lax.Precision.HI...]
    convert_element_type x13 -> x3, other arithmetic: 7.22 us -> 1.65 us  [the longest x1 1.62 us: local(): du = two(high_join, du.astype(BF))]
  transfers between devices with their start and end apart: 35 -> 58, of which waited for: 15 -> 27; matrix products, arithmetic and copies ran while one was open for 9% -> 4% of each run, Pallas kernels for 8% -> 30%
where the time goes in v2:
time: 336 us; the launch traced here: 329 us
  Pallas kernels  153 us (46%)
  waiting for transfers between devices  97.2 us (29%)
  starting transfers between devices  54.6 us (16%)
  local copies, waits for them, and re-layouts  11 us (3%)
  other arithmetic  10.8 us (3%)
    pallas_call x14, Pallas kernels, call(): pl.pallas_call(kernel, out_shape=outs, in_specs=[pl.BlockSpec(memory_spac...  153 us
    ppermute x58, waiting for transfers between devices, swap(): return lax.ppermute(value, axis, [(i, i ^ bit) for i in range(size)])  97.2 us
    ppermute x58, starting transfers between devices, swap(): return lax.ppermute(value, axis, [(i, i ^ bit) for i in range(size)])  54.6 us
  transfers between devices with their start and end apart: 58, of which 27 were waited for; matrix products, arithmetic and copies ran while one was open for 4% of the time, Pallas kernels for 30%

profile of v2, /device:TPU:0, one launch (start us, length us, event | category | flops | bytes accessed | tf_op | source)
XLA Modules:
  0.0 329.1 jit_solution(8624967144632229698)
XLA Ops:
  1.2 2.1 bitcast_select_fusion
  3.3 2.6 collective-permute-start
  7.6 2.3 select_select_fusion
  9.9 3.8 %collective-permute-done.refs_3_.refs_2_ = bf16[192,768]{1,0:T(8,128)(2,1)} collective-permute-done((bf16[192,768]{1,0:T(8,128)(2,1)S(1)}, bf16[192,768]{1,0:T(8,128)(2,1)}, u32[]{:S(2)}, u32[]{:S(2)}) %collective-permute-start) | collective-permute-done | bytes 294944 | tf_op jit(solution)/shard_map/ppermute | solution.py:650
  13.6 1.8 collective-permute-start.5
  15.5 1.6 collective-permute-start.6
  17.1 1.6 collective-permute-start.7
  19.8 1.5 collective-permute-start.4
  21.3 11.5 %shard_map.331 = (bf16[768,768]{1,0:T(8,128)(2,1)}, bf16[768,1152]{1,0:T(8,128)(2,1)}, f32[18,256,128]{2,1,0:T(8,128)}, bf16[768,384]{1,0:T(8,128)(2,1)}, f32[768,768]{1,0:T(8,128)}) custom-call(s32[6]{0:T(128)} %dynamic_slice.9.refs_0_, bf16[768,768]{1,0:T(8,128)(2,1)} %refs_14_.2, f32[8,768]{1,0:T(8,128)} %pad.16.refs_2_.refs_15_, ...), custom_call_target="tpu_custom_call" | custom-call | flops 1962934272 | bytes 11870232 | tf_op jit(solution)/shard_map/pallas_call | solution.py:114
  32.8 2.9 collective-permute-done.4.refs_11_.refs_10_
  37.0 1.8 collective-permute-done.13.refs_12_.refs_11_
  40.6 1.5 collective-permute-start.16
  44.4 1.6 collective-permute-start.17
  46.0 14.2 %shard_map.332 = (bf16[768,1152]{1,0:T(8,128)(2,1)}, f32[18,256,128]{2,1,0:T(8,128)}, bf16[768,384]{1,0:T(8,128)(2,1)}, f32[768,768]{1,0:T(8,128)}, bf16[768,768]{1,0:T(8,128)(2,1)}) custom-call(s32[6]{0:T(128)} %dynamic_slice.9.refs_0_, s32[1]{0:T(128)} %bitcast.refs_1_.refs_0_, bf16[768,768]{1,0:T(8,128)(2,1)} %get-tuple-element.192.refs_2_.refs_13_.refs_7_, ...), custom_call_target="tpu_custom_call" | custom-call | flops 1962934272 | bytes 15413788 | tf_op jit(solution)/shard_map/pallas_call | solution.py:114
  61.4 12.2 %shard_map.333 = (bf16[768,768]{1,0:T(8,128)(2,1)}, bf16[768,768]{1,0:T(8,128)(2,1)}, f32[768,768]{1,0:T(8,128)}, f32[768,768]{1,0:T(8,128)}, f32[768,768]{1,0:T(8,128)}) custom-call(bf16[768,768]{1,0:T(8,128)(2,1)} %get-tuple-element.206.refs_0_.refs_1_.refs_4_, bf16[768,768]{1,0:T(8,128)(2,1)} %refs_9_.1, ...), custom_call_target="tpu_custom_call" | custom-call | flops 3623878656 | bytes 15384576 | tf_op jit(solution)/shard_map/pallas_call | solution.py:114
  75.0 23.7 %shard_map.334 = (bf16[768,768]{1,0:T(8,128)(2,1)}, bf16[768,768]{1,0:T(8,128)(2,1)}, f32[768,768]{1,0:T(8,128)}, f32[768,768]{1,0:T(8,128)}, f32[1,768]{1,0:T(1...) custom-call(s32[1]{0:T(128)} %bitcast.refs_1_.refs_0_, ...), custom_call_target="tpu_custom_call" | custom-call | flops 10871635968 | bytes 24860164 | tf_op jit(solution)/shard_map/pallas_call | solution.py:114
  99.9 2.0 collective-permute-done.23.refs_2_
  101.8 1.7 collective-permute-done.24.refs_4_
  104.5 5.3 %shard_map.335 = (f32[384,768]{1,0:T(8,128)}, bf16[384,768]{1,0:T(8,128)(2,1)}, f32[384,768]{1,0:T(8,128)}, bf16[384,768]{1,0:T(8,128)(2,1)}) custom-call(s32[3]{0:T(128)} %pad_add_fusion.refs_0_, f32[768,768]{1,0:T(8,128)} %get-tuple-element.222.refs_1_, bf16[768,768]{1,0:T(8,128)(2,1)} %copy-done.7, f32[768,768]{1,0:T(8,128)} %get-tuple-element.224.refs_3_, ...), custom_call_target="tpu_custom_call" | custom-call | flops 1 | bytes 10616844 | tf_op jit(solution)/shard_map/pallas_call | solution.py:114
  111.8 18.8 %shard_map.336 = (bf16[768,768]{1,0:T(8,128)(2,1)}, bf16[768,768]{1,0:T(8,128)(2,1)}, f32[768,768]{1,0:T(8,128)}, f32[768,768]{1,0:T(8,128)}, f32[1,768]{1,0:T(1...) custom-call(f32[768,768]{1,0:T(8,128)} %get-tuple-element.230.refs_0_, ...), custom_call_target="tpu_custom_call" | custom-call | flops 7247757312 | bytes 29523456 | tf_op jit(solution)/shard_map/pallas_call | solution.py:114
  131.2 2.5 collective-permute-done.27.refs_2_
  133.8 1.7 collective-permute-done.28.refs_4_
  136.5 7.2 %shard_map.337 = (f32[384,768]{1,0:T(8,128)}, f32[384,768]{1,0:T(8,128)}, f32[192,768]{1,0:T(8,128)}, f32[192,768]{1,0:T(8,128)}, bf16[576,768]{1,0:T(8,128)(2,1)}, /*index=5*/bf16[576,768]{1,0:T(8,128)(2,1)}) custom-call(s32[3]{0:T(128)} %pad_add_fusion.refs_0_, f32[768,768]{1,0:T(8,128)} %get-tuple-element.242.refs_1_, bf16[768,768]{1,0:T(8,128)(2,1)} %copy-done.10, ...), custom_call_target="tpu_custom_call" | custom-call | flops 1 | bytes 15925260 | tf_op jit(solution)/shard_map/pallas_call | solution.py:114
  145.9 16.9 %shard_map.338 = (bf16[768,768]{1,0:T(8,128)(2,1)}, f32[768,768]{1,0:T(8,128)}, f32[8,384]{1,0:T(8,128)}, f32[768,768]{1,0:T(8,128)}) custom-call(s32[1]{0:T(128)} %bitcast.refs_1_.refs_0_, f32[768,768]{1,0:T(8,128)} %get-tuple-element.281.refs_1_, bf16[192,768]{1,0:T(8,128)(2,1)} %collective-permute-done.refs_3_.refs_2_, ...), custom_call_target="tpu_custom_call" | custom-call | flops 3925868544 | bytes 16527364 | tf_op jit(solution)/shard_map/pallas_call | solution.py:114
  162.8 2.8 collective-permute-done.29.refs_7_
  166.3 3.1 collective-permute-done.31.refs_2_
  170.3 6.4 %shard_map.339 = (bf16[384,768]{1,0:T(8,128)(2,1)}, bf16[384,768]{1,0:T(8,128)(2,1)}, f32[192,768]{1,0:T(8,128)}, bf16[192,768]{1,0:T(8,128)(2,1)}, f32[192,768]...) custom-call(s32[3]{0:T(128)} %pad_add_fusion.refs_0_, ...), custom_call_target="tpu_custom_call" | custom-call | flops 1 | bytes 12681228 | tf_op jit(solution)/shard_map/pallas_call | solution.py:114
  180.3 2.6 collective-permute-start.35
  182.9 16.3 %shard_map.340 = (bf16[768,768]{1,0:T(8,128)(2,1)}, f32[768,768]{1,0:T(8,128)}, f32[768,768]{1,0:T(8,128)}, f32[32,768]{1,0:T(8,128)}) custom-call(s32[1]{0:T(128)} %bitcast.7.refs_0_, f32[768,768]{1,0:T(8,128)} %get-tuple-element.281.refs_1_, bf16[192,768]{1,0:T(8,128)(2,1)} %refs_2_.2, bf16[192,768]{1,0:T(8,128)(2,1)} %copy-done.38, ...), custom_call_target="tpu_custom_call" | custom-call | flops 3925868544 | bytes 19049476 | tf_op jit(solution)/shard_map/pallas_call | solution.py:114
  200.7 3.5 %shard_map.341 = (f32[192,768]{1,0:T(8,128)}, bf16[192,768]{1,0:T(8,128)(2,1)}, bf16[192,768]{1,0:T(8,128)(2,1)}) custom-call(s32[3]{0:T(128)} %pad_add_fusion.refs_0_, f32[192,768]{1,0:T(8,128)} %get-tuple-element.305.refs_1_, bf16[192,768]{1,0:T(8,128)(2,1)} %copy-done.23, f32[192,768]{1,0:T(8,128)} %get-tuple-element.307.refs_3_, ...), custom_call_target="tpu_custom_call" | custom-call | flops 1 | bytes 3833868 | tf_op jit(solution)/shard_map/pallas_call | solution.py:114
  206.7 14.0 %collective-permute-done.39 = bf16[192,768]{1,0:T(8,128)(2,1)S(1)} collective-permute-done((bf16[192,768]{1,0:T(8,128)(2,1)}, bf16[192,768]{1,0:T(8,128)(2,1)S(1)}, u32[]{:S(2)}, u32[]{:S(2)}) %collective-permute-start.39) | collective-permute-done | bytes 294944 | tf_op jit(solution)/shard_map/ppermute | solution.py:650
  221.7 1.6 add_convert_fusion
  223.8 4.7 %shard_map.342 = (f32[192,768]{1,0:T(8,128)}, bf16[192,768]{1,0:T(8,128)(2,1)}, bf16[192,768]{1,0:T(8,128)(2,1)}, bf16[192,768]{1,0:T(8,128)(2,1)}) custom-call(s32[3]{0:T(128)} %pad_add_fusion.refs_0_, f32[768,768]{1,0:T(8,128)} %get-tuple-element.294.refs_1_, bf16[768,768]{1,0:T(8,128)(2,1)} %copy-done.6, bf16[384,768]{1,0:T(8,128)(2,1)} %copy-done.14, ...), custom_call_target="tpu_custom_call" | custom-call | flops 1 | bytes 6193164 | tf_op jit(solution)/shard_map/pallas_call | solution.py:114
  233.3 3.7 %collective-permute-done.41 = f32[40,768]{1,0:T(8,128)S(1)} collective-permute-done((f32[40,768]{1,0:T(8,128)S(1)}, f32[40,768]{1,0:T(8,128)S(1)}, u32[]{:S(2)}, u32[]{:S(2)}) %collective-permute-start.41) | collective-permute-done | bytes 122912 | tf_op jit(solution)/shard_map/ppermute | solution.py:650
  237.0 2.3 collective-permute-done.42
  239.3 5.9 %collective-permute-done.44 = bf16[192,768]{1,0:T(8,128)(2,1)S(1)} collective-permute-done((bf16[192,768]{1,0:T(8,128)(2,1)}, bf16[192,768]{1,0:T(8,128)(2,1)S(1)}, u32[]{:S(2)}, u32[]{:S(2)}) %collective-permute-start.44) | collective-permute-done | bytes 294944 | tf_op jit(solution)/shard_map/ppermute | solution.py:650
  245.2 5.1 %collective-permute-done.45 = bf16[192,768]{1,0:T(8,128)(2,1)S(1)} collective-permute-done((bf16[192,768]{1,0:T(8,128)(2,1)}, bf16[192,768]{1,0:T(8,128)(2,1)S(1)}, u32[]{:S(2)}, u32[]{:S(2)}) %collective-permute-start.45) | collective-permute-done | bytes 294944 | tf_op jit(solution)/shard_map/ppermute | solution.py:650
  252.9 3.4 %collective-permute-start.46 = (bf16[96,768]{1,0:T(8,128)(2,1)S(1)}, bf16[96,768]{1,0:T(8,128)(2,1)S(1)}, u32[]{:S(2)}, u32[]{:S(2)}) collective-permute-start(bf16[96,768]{1,0:T(8,128)(2,1)S(1)} %dynamic-slice_convert_fusion), channel_id=1, source_target_pairs={{0,16},{4,20},{8,24},{12,28},{16,0},{20,4},{24,8},{28,12},{1,17},{... | collective-permute-start | bytes 442376 | tf_op jit(solution)/shard_map/ppermute | solution.py:650
  257.8 2.4 collective-permute-done.46
  262.6 3.3 %collective-permute-start.53 = (f32[88,768]{1,0:T(8,128)S(1)}, f32[88,768]{1,0:T(8,128)S(1)}, u32[]{:S(2)}, u32[]{:S(2)}) collective-permute-start(f32[88,768]{1,0:T(8,128)S(1)} %pad_maximum_fusion.8), channel_id=1, source_target_pairs={{0,8},{4,12},{8,0},{12,4},{16,24},{20,28},{24,16},{28,20},{1,9},{5... | collective-permute-start | bytes 811016 | tf_op jit(solution)/shard_map/ppermute | solution.py:650
  267.6 1.8 collective-permute-start.50
  269.4 7.1 %collective-permute-done.53 = f32[88,768]{1,0:T(8,128)S(1)} collective-permute-done((f32[88,768]{1,0:T(8,128)S(1)}, f32[88,768]{1,0:T(8,128)S(1)}, u32[]{:S(2)}, u32[]{:S(2)}) %collective-permute-start.53) | collective-permute-done | bytes 270368 | tf_op jit(solution)/shard_map/ppermute | solution.py:650
  276.6 9.9 %collective-permute-done.50 = bf16[96,768]{1,0:T(8,128)(2,1)S(1)} collective-permute-done((bf16[96,768]{1,0:T(8,128)(2,1)S(1)}, bf16[96,768]{1,0:T(8,128)(2,1)S(1)}, u32[]{:S(2)}, u32[]{:S(2)}) %collective-permute-start.50) | collective-permute-done | bytes 147488 | tf_op jit(solution)/shard_map/ppermute | solution.py:650
  287.3 2.7 collective-permute-start.54
  293.6 15.5 %collective-permute-done.54 = f32[152,768]{1,0:T(8,128)S(1)} collective-permute-done((f32[152,768]{1,0:T(8,128)S(1)}, f32[152,768]{1,0:T(8,128)S(1)}, u32[]{:S(2)}, u32[]{:S(2)}) %collective-permute-start.54) | collective-permute-done | bytes 466976 | tf_op jit(solution)/shard_map/ppermute | solution.py:650
  312.2 1.5 slice_add_fusion.refs_6_
  314.5 5.0 %shard_map.344 = (f32[768,768]{1,0:T(8,128)}, f32[768,768]{1,0:T(8,128)}, f32[576,768]{1,0:T(8,128)}, f32[192,768]{1,0:T(8,128)}) custom-call(s32[3]{0:T(128)} %pad_add_fusion.refs_0_, bf16[384,768]{1,0:T(8,128)(2,1)} %copy-done.2, bf16[384,768]{1,0:T(8,128)(2,1)} %copy-done.18, bf16[384,768]{1,0:T(8,128)(2,1)} %copy-done.1, bf16[384,768]{1,0:T(8,128)(2,1)} %copy-done.17, ...), custom_call_target="tpu_custom_call" | custom-call | flops 1 | bytes 10616844 | tf_op jit(solution)/shard_map/pallas_call | solution.py:114
  319.5 7.4 %shard_map.343 = (f32[128,512]{1,0:T(8,128)}, f32[512]{0:T(512)}, f32[512,768]{1,0:T(8,128)}, f32[768]{0:T(1024)}, f32[768]{0:T(1024)}, /*index=5*/f32[768]{0:T(...) custom-call(s32[1]{0:T(128)} %bitcast.7.refs_0_, ...), custom_call_target="tpu_custom_call" | custom-call | flops 1 | bytes 3548164 | tf_op jit(solution)/shard_map/pallas_call | solution.py:114
  (232 shorter events, 52.5 us)
Async XLA Ops:
  0.7 17.9 %collective-permute-start.3 = (bf16[192,768]{1,0:T(8,128)(2,1)}, bf16[192,768]{1,0:T(8,128)(2,1)S(1)}, u32[]{:S(2)}, u32[]{:S(2)}) collective-permute-start(bf16[192,768]{1,0:T(8,128)(2,1)} %refs_2_.2), channel_id=1, source_target_pairs={{0,1},{1,0},{2,3},{3,2},{4,5},{5,4},{6,7},{7,6},{8,9},{9,8},{10,11... | collective-permute-start | bytes 884744 | tf_op jit(solution)/shard_map/ppermute | solution.py:650
  3.3 10.3 %collective-permute-start = (bf16[192,768]{1,0:T(8,128)(2,1)S(1)}, bf16[192,768]{1,0:T(8,128)(2,1)}, u32[]{:S(2)}, u32[]{:S(2)}) collective-permute-start(bf16[192,768]{1,0:T(8,128)(2,1)S(1)} %get-tuple-element.366), channel_id=1, source_target_pairs={{0,2},{1,3},{2,0},{3,1},{4,6},{5,7},{6,4},{7,5},{8,10},{9,11},{10,... | collective-permute-start | bytes 884744 | tf_op jit(solution)/shard_map/ppermute | solution.py:650
  5.9 13.8 %collective-permute-start.1 = (bf16[576,768]{1,0:T(8,128)(2,1)}, bf16[576,768]{1,0:T(8,128)(2,1)}, u32[]{:S(2)}, u32[]{:S(2)}) collective-permute-start(bf16[576,768]{1,0:T(8,128)(2,1)} %bitcast.5.refs_3_.refs_8_), channel_id=1, source_target_pairs={{0,1},{1,0},{2,3},{3,2},{4,5},{5,4},{6,7},{7,6},{8,9},{9,8},{10,11... | collective-permute-start | bytes 2654216 | tf_op jit(solution)/shard_map/ppermute | solution.py:650
  13.6 22.7 %collective-permute-start.5 = (bf16[384,768]{1,0:T(8,128)(2,1)}, bf16[384,768]{1,0:T(8,128)(2,1)}, u32[]{:S(2)}, u32[]{:S(2)}) collective-permute-start(bf16[384,768]{1,0:T(8,128)(2,1)} %get-tuple-element.194), channel_id=1, source_target_pairs={{0,2},{1,3},{2,0},{3,1},{4,6},{5,7},{6,4},{7,5},{8,10},{9,11},{10,... | collective-permute-start | bytes 1769480 | tf_op jit(solution)/shard_map/ppermute | solution.py:650
  15.5 20.3 %collective-permute-start.6 = (bf16[192,768]{1,0:T(8,128)(2,1)}, bf16[192,768]{1,0:T(8,128)(2,1)}, u32[]{:S(2)}, u32[]{:S(2)}) collective-permute-start(bf16[192,768]{1,0:T(8,128)(2,1)} %collective-permute-done.refs_3_.refs_2_), channel_id=1, source_target_pairs={{0,4},{4,0},{8,12},{12,8},{16,20},{20,16},{24,28},{28,24},{1,5},{5... | collective-permute-start | bytes 884744 | tf_op jit(solution)/shard_map/ppermute | solution.py:650
  17.1 19.2 %collective-permute-start.7 = (bf16[192,768]{1,0:T(8,128)(2,1)}, bf16[192,768]{1,0:T(8,128)(2,1)}, u32[]{:S(2)}, u32[]{:S(2)}) collective-permute-start(bf16[192,768]{1,0:T(8,128)(2,1)} %collective-permute-done.refs_3_.refs_2_), channel_id=1, source_target_pairs={{0,8},{4,12},{8,0},{12,4},{16,24},{20,28},{24,16},{28,20},{1,9},{5... | collective-permute-start | bytes 884744 | tf_op jit(solution)/shard_map/ppermute | solution.py:650
  18.7 17.6 %collective-permute-start.8 = (bf16[192,768]{1,0:T(8,128)(2,1)}, bf16[192,768]{1,0:T(8,128)(2,1)}, u32[]{:S(2)}, u32[]{:S(2)}) collective-permute-start(bf16[192,768]{1,0:T(8,128)(2,1)} %get-tuple-element.196), channel_id=1, source_target_pairs={{0,2},{1,3},{2,0},{3,1},{4,6},{5,7},{6,4},{7,5},{8,10},{9,11},{10,... | collective-permute-start | bytes 884744 | tf_op jit(solution)/shard_map/ppermute | solution.py:650
  19.8 16.0 %collective-permute-start.4 = (bf16[16,768]{1,0:T(8,128)(2,1)S(1)}, bf16[16,768]{1,0:T(8,128)(2,1)S(1)}, u32[]{:S(2)}, u32[]{:S(2)}) collective-permute-start(bf16[16,768]{1,0:T(8,128)(2,1)S(1)} %fusion.2.refs_5_), channel_id=1, source_target_pairs={{0,2},{1,3},{2,0},{3,1},{4,6},{5,7},{6,4},{7,5},{8,10},{9,11},{10,... | collective-permute-start | bytes 73736 | tf_op jit(solution)/shard_map/ppermute | solution.py:650
  35.8 24.4 %collective-permute-start.14 = (bf16[768,768]{1,0:T(8,128)(2,1)S(1)}, bf16[768,768]{1,0:T(8,128)(2,1)}, u32[]{:S(2)}, u32[]{:S(2)}) collective-permute-start(bf16[768,768]{1,0:T(8,128)(2,1)S(1)} %copy-done.4), channel_id=1, source_target_pairs={{0,1},{1,0},{2,3},{3,2},{4,5},{5,4},{6,7},{7,6},{8,9},{9,8},{10,11... | collective-permute-start | bytes 3538952 | tf_op jit(solution)/shard_map/ppermute | solution.py:650
  35.8 24.4 %collective-permute-start.15 = (bf16[768,768]{1,0:T(8,128)(2,1)S(1)}, bf16[768,768]{1,0:T(8,128)(2,1)}, u32[]{:S(2)}, u32[]{:S(2)}) collective-permute-start(bf16[768,768]{1,0:T(8,128)(2,1)S(1)} %copy-done.5), channel_id=1, source_target_pairs={{0,1},{1,0},{2,3},{3,2},{4,5},{5,4},{6,7},{7,6},{8,9},{9,8},{10,11... | collective-permute-start | bytes 3538952 | tf_op jit(solution)/shard_map/ppermute | solution.py:650
  40.6 19.7 %collective-permute-start.16 = (bf16[384,768]{1,0:T(8,128)(2,1)}, bf16[384,768]{1,0:T(8,128)(2,1)S(1)}, u32[]{:S(2)}, u32[]{:S(2)}) collective-permute-start(bf16[384,768]{1,0:T(8,128)(2,1)} %collective-permute-done.5.refs_2_), channel_id=1, source_target_pairs={{0,4},{4,0},{8,12},{12,8},{16,20},{20,16},{24,28},{28,24},{1,5},{5... | collective-permute-start | bytes 1769480 | tf_op jit(solution)/shard_map/ppermute | solution.py:650
  42.1 18.1 %collective-permute-start.18 = (bf16[384,768]{1,0:T(8,128)(2,1)S(1)}, bf16[384,768]{1,0:T(8,128)(2,1)}, u32[]{:S(2)}, u32[]{:S(2)}) collective-permute-start(bf16[384,768]{1,0:T(8,128)(2,1)S(1)} %get-tuple-element.205), channel_id=1, source_target_pairs={{0,2},{1,3},{2,0},{3,1},{4,6},{5,7},{6,4},{7,5},{8,10},{9,11},{10,... | collective-permute-start | bytes 1769480 | tf_op jit(solution)/shard_map/ppermute | solution.py:650
  44.4 15.9 %collective-permute-start.17 = (bf16[384,768]{1,0:T(8,128)(2,1)}, bf16[384,768]{1,0:T(8,128)(2,1)}, u32[]{:S(2)}, u32[]{:S(2)}) collective-permute-start(bf16[384,768]{1,0:T(8,128)(2,1)} %collective-permute-done.5.refs_2_), channel_id=1, source_target_pairs={{0,8},{4,12},{8,0},{12,4},{16,24},{20,28},{24,16},{28,20},{1,9},{5... | collective-permute-start | bytes 1769480 | tf_op jit(solution)/shard_map/ppermute | solution.py:650
  60.3 13.3 %collective-permute-start.19 = (bf16[384,768]{1,0:T(8,128)(2,1)}, bf16[384,768]{1,0:T(8,128)(2,1)S(1)}, u32[]{:S(2)}, u32[]{:S(2)}) collective-permute-start(bf16[384,768]{1,0:T(8,128)(2,1)} %collective-permute-done.5.refs_2_), channel_id=1, source_target_pairs={{0,1},{1,0},{2,3},{3,2},{4,5},{5,4},{6,7},{7,6},{8,9},{9,8},{10,11... | collective-permute-start | bytes 1769480 | tf_op jit(solution)/shard_map/ppermute | solution.py:650
  60.3 13.3 %collective-permute-start.20 = (bf16[384,768]{1,0:T(8,128)(2,1)S(1)}, bf16[384,768]{1,0:T(8,128)(2,1)S(1)}, u32[]{:S(2)}, u32[]{:S(2)}) collective-permute-start(bf16[384,768]{1,0:T(8,128)(2,1)S(1)} %collective-permute-done.16.refs_3_), channel_id=1, source_target_pairs={{0,1},{1,0},{2,3},{3,2},{4,5},{5,4},{6,7},{7,6},{8,9},{9,8},{10,11... | collective-permute-start | bytes 1769480 | tf_op jit(solution)/shard_map/ppermute | solution.py:650
  60.8 12.8 %collective-permute-start.21 = (bf16[384,768]{1,0:T(8,128)(2,1)}, bf16[384,768]{1,0:T(8,128)(2,1)S(1)}, u32[]{:S(2)}, u32[]{:S(2)}) collective-permute-start(bf16[384,768]{1,0:T(8,128)(2,1)} %collective-permute-done.17.refs_4_), channel_id=1, source_target_pairs={{0,1},{1,0},{2,3},{3,2},{4,5},{5,4},{6,7},{7,6},{8,9},{9,8},{10,11... | collective-permute-start | bytes 1769480 | tf_op jit(solution)/shard_map/ppermute | solution.py:650
  60.9 12.7 %collective-permute-start.22 = (bf16[384,768]{1,0:T(8,128)(2,1)}, bf16[384,768]{1,0:T(8,128)(2,1)S(1)}, u32[]{:S(2)}, u32[]{:S(2)}) collective-permute-start(bf16[384,768]{1,0:T(8,128)(2,1)} %collective-permute-done.18.refs_5_), channel_id=1, source_target_pairs={{0,1},{1,0},{2,3},{3,2},{4,5},{5,4},{6,7},{7,6},{8,9},{9,8},{10,11... | collective-permute-start | bytes 1769480 | tf_op jit(solution)/shard_map/ppermute | solution.py:650
  98.8 4.7 %collective-permute-start.24 = (bf16[768,768]{1,0:T(8,128)(2,1)}, bf16[768,768]{1,0:T(8,128)(2,1)S(1)}, u32[]{:S(2)}, u32[]{:S(2)}) collective-permute-start(bf16[768,768]{1,0:T(8,128)(2,1)} %get-tuple-element.225), channel_id=1, source_target_pairs={{0,1},{1,0},{2,3},{3,2},{4,5},{5,4},{6,7},{7,6},{8,9},{9,8},{10,11... | collective-permute-start | bytes 3538952 | tf_op jit(solution)/shard_map/ppermute | solution.py:650
  109.9 20.7 %collective-permute-start.25 = (bf16[384,768]{1,0:T(8,128)(2,1)}, bf16[384,768]{1,0:T(8,128)(2,1)S(1)}, u32[]{:S(2)}, u32[]{:S(2)}) collective-permute-start(bf16[384,768]{1,0:T(8,128)(2,1)} %get-tuple-element.239), channel_id=1, source_target_pairs={{0,4},{4,0},{8,12},{12,8},{16,20},{20,16},{24,28},{28,24},{1,5},{5... | collective-permute-start | bytes 1769480 | tf_op jit(solution)/shard_map/ppermute | solution.py:650
  110.8 19.8 %collective-permute-start.26 = (bf16[384,768]{1,0:T(8,128)(2,1)}, bf16[384,768]{1,0:T(8,128)(2,1)S(1)}, u32[]{:S(2)}, u32[]{:S(2)}) collective-permute-start(bf16[384,768]{1,0:T(8,128)(2,1)} %get-tuple-element.240), channel_id=1, source_target_pairs={{0,8},{4,12},{8,0},{12,4},{16,24},{20,28},{24,16},{28,20},{1,9},{5... | collective-permute-start | bytes 1769480 | tf_op jit(solution)/shard_map/ppermute | solution.py:650
  130.7 4.7 %collective-permute-start.28 = (bf16[768,768]{1,0:T(8,128)(2,1)}, bf16[768,768]{1,0:T(8,128)(2,1)S(1)}, u32[]{:S(2)}, u32[]{:S(2)}) collective-permute-start(bf16[768,768]{1,0:T(8,128)(2,1)} %get-tuple-element.245), channel_id=1, source_target_pairs={{0,1},{1,0},{2,3},{3,2},{4,5},{5,4},{6,7},{7,6},{8,9},{9,8},{10,11... | collective-permute-start | bytes 3538952 | tf_op jit(solution)/shard_map/ppermute | solution.py:650
  143.7 22.0 %collective-permute-start.29 = (bf16[576,768]{1,0:T(8,128)(2,1)}, bf16[576,768]{1,0:T(8,128)(2,1)S(1)}, u32[]{:S(2)}, u32[]{:S(2)}) collective-permute-start(bf16[576,768]{1,0:T(8,128)(2,1)} %get-tuple-element.263), channel_id=1, source_target_pairs={{0,4},{4,0},{8,12},{12,8},{16,20},{20,16},{24,28},{28,24},{1,5},{5... | collective-permute-start | bytes 2654216 | tf_op jit(solution)/shard_map/ppermute | solution.py:650
  144.6 21.6 %collective-permute-start.30 = (bf16[576,768]{1,0:T(8,128)(2,1)}, bf16[576,768]{1,0:T(8,128)(2,1)S(1)}, u32[]{:S(2)}, u32[]{:S(2)}) collective-permute-start(bf16[576,768]{1,0:T(8,128)(2,1)} %get-tuple-element.264), channel_id=1, source_target_pairs={{0,8},{4,12},{8,0},{12,4},{16,24},{20,28},{24,16},{28,20},{1,9},{5... | collective-permute-start | bytes 2654216 | tf_op jit(solution)/shard_map/ppermute | solution.py:650
  176.7 22.5 %collective-permute-start.32 = (bf16[384,768]{1,0:T(8,128)(2,1)}, bf16[384,768]{1,0:T(8,128)(2,1)S(1)}, u32[]{:S(2)}, u32[]{:S(2)}) collective-permute-start(bf16[384,768]{1,0:T(8,128)(2,1)} %get-tuple-element.298), channel_id=1, source_target_pairs={{0,2},{1,3},{2,0},{3,1},{4,6},{5,7},{6,4},{7,5},{8,10},{9,11},{10,... | collective-permute-start | bytes 1769480 | tf_op jit(solution)/shard_map/ppermute | solution.py:650
  178.3 20.9 %collective-permute-start.33 = (bf16[192,768]{1,0:T(8,128)(2,1)}, bf16[192,768]{1,0:T(8,128)(2,1)S(1)}, u32[]{:S(2)}, u32[]{:S(2)}) collective-permute-start(bf16[192,768]{1,0:T(8,128)(2,1)} %get-tuple-element.299), channel_id=1, source_target_pairs={{0,8},{4,12},{8,0},{12,4},{16,24},{20,28},{24,16},{28,20},{1,9},{5... | collective-permute-start | bytes 884744 | tf_op jit(solution)/shard_map/ppermute | solution.py:650
  179.3 19.9 %collective-permute-start.34 = (bf16[192,768]{1,0:T(8,128)(2,1)}, bf16[192,768]{1,0:T(8,128)(2,1)S(1)}, u32[]{:S(2)}, u32[]{:S(2)}) collective-permute-start(bf16[192,768]{1,0:T(8,128)(2,1)} %get-tuple-element.300), channel_id=1, source_target_pairs={{0,4},{4,0},{8,12},{12,8},{16,20},{20,16},{24,28},{28,24},{1,5},{5... | collective-permute-start | bytes 884744 | tf_op jit(solution)/shard_map/ppermute | solution.py:650
  180.3 18.9 %collective-permute-start.35 = (bf16[192,768]{1,0:T(8,128)(2,1)}, bf16[192,768]{1,0:T(8,128)(2,1)S(1)}, u32[]{:S(2)}, u32[]{:S(2)}) collective-permute-start(bf16[192,768]{1,0:T(8,128)(2,1)} %get-tuple-element.301), channel_id=1, source_target_pairs={{0,16},{4,20},{8,24},{12,28},{16,0},{20,4},{24,8},{28,12},{1,17},{... | collective-permute-start | bytes 884744 | tf_op jit(solution)/shard_map/ppermute | solution.py:650
  199.3 22.4 %collective-permute-start.36 = (bf16[768,768]{1,0:T(8,128)(2,1)}, bf16[768,768]{1,0:T(8,128)(2,1)S(1)}, u32[]{:S(2)}, u32[]{:S(2)}) collective-permute-start(bf16[768,768]{1,0:T(8,128)(2,1)} %get-tuple-element.302), channel_id=1, source_target_pairs={{0,1},{1,0},{2,3},{3,2},{4,5},{5,4},{6,7},{7,6},{8,9},{9,8},{10,11... | collective-permute-start | bytes 3538952 | tf_op jit(solution)/shard_map/ppermute | solution.py:650
  199.4 22.3 %collective-permute-start.38 = (bf16[384,768]{1,0:T(8,128)(2,1)}, bf16[384,768]{1,0:T(8,128)(2,1)S(1)}, u32[]{:S(2)}, u32[]{:S(2)}) collective-permute-start(bf16[384,768]{1,0:T(8,128)(2,1)} %get-tuple-element.304), channel_id=1, source_target_pairs={{0,2},{1,3},{2,0},{3,1},{4,6},{5,7},{6,4},{7,5},{8,10},{9,11},{10,... | collective-permute-start | bytes 1769480 | tf_op jit(solution)/shard_map/ppermute | solution.py:650
  204.2 16.6 %collective-permute-start.39 = (bf16[192,768]{1,0:T(8,128)(2,1)}, bf16[192,768]{1,0:T(8,128)(2,1)S(1)}, u32[]{:S(2)}, u32[]{:S(2)}) collective-permute-start(bf16[192,768]{1,0:T(8,128)(2,1)} %get-tuple-element.312), channel_id=1, source_target_pairs={{0,16},{4,20},{8,24},{12,28},{16,0},{20,4},{24,8},{28,12},{1,17},{... | collective-permute-start | bytes 884744 | tf_op jit(solution)/shard_map/ppermute | solution.py:650
  204.6 17.1 %collective-permute-start.40 = (bf16[192,768]{1,0:T(8,128)(2,1)}, bf16[192,768]{1,0:T(8,128)(2,1)S(1)}, u32[]{:S(2)}, u32[]{:S(2)}) collective-permute-start(bf16[192,768]{1,0:T(8,128)(2,1)} %get-tuple-element.313), channel_id=1, source_target_pairs={{0,2},{1,3},{2,0},{3,1},{4,6},{5,7},{6,4},{7,5},{8,10},{9,11},{10,... | collective-permute-start | bytes 884744 | tf_op jit(solution)/shard_map/ppermute | solution.py:650
  223.3 16.0 %collective-permute-start.42 = (bf16[192,768]{1,0:T(8,128)(2,1)S(1)}, bf16[192,768]{1,0:T(8,128)(2,1)S(1)}, u32[]{:S(2)}, u32[]{:S(2)}) collective-permute-start(bf16[192,768]{1,0:T(8,128)(2,1)S(1)} %add_convert_fusion), channel_id=1, source_target_pairs={{0,16},{4,20},{8,24},{12,28},{16,0},{20,4},{24,8},{28,12},{1,17},{... | collective-permute-start | bytes 884744 | tf_op jit(solution)/shard_map/ppermute | solution.py:650
  228.5 10.8 %collective-permute-start.43 = (bf16[192,768]{1,0:T(8,128)(2,1)}, bf16[192,768]{1,0:T(8,128)(2,1)S(1)}, u32[]{:S(2)}, u32[]{:S(2)}) collective-permute-start(bf16[192,768]{1,0:T(8,128)(2,1)} %get-tuple-element.322), channel_id=1, source_target_pairs={{0,4},{4,0},{8,12},{12,8},{16,20},{20,16},{24,28},{28,24},{1,5},{5... | collective-permute-start | bytes 884744 | tf_op jit(solution)/shard_map/ppermute | solution.py:650
  229.6 15.6 %collective-permute-start.44 = (bf16[192,768]{1,0:T(8,128)(2,1)}, bf16[192,768]{1,0:T(8,128)(2,1)S(1)}, u32[]{:S(2)}, u32[]{:S(2)}) collective-permute-start(bf16[192,768]{1,0:T(8,128)(2,1)} %get-tuple-element.323), channel_id=1, source_target_pairs={{0,8},{4,12},{8,0},{12,4},{16,24},{20,28},{24,16},{28,20},{1,9},{5... | collective-permute-start | bytes 884744 | tf_op jit(solution)/shard_map/ppermute | solution.py:650
  230.6 19.7 %collective-permute-start.45 = (bf16[192,768]{1,0:T(8,128)(2,1)}, bf16[192,768]{1,0:T(8,128)(2,1)S(1)}, u32[]{:S(2)}, u32[]{:S(2)}) collective-permute-start(bf16[192,768]{1,0:T(8,128)(2,1)} %get-tuple-element.324), channel_id=1, source_target_pairs={{0,12},{4,8},{8,4},{12,0},{16,28},{20,24},{24,20},{28,16},{1,13},{... | collective-permute-start | bytes 884744 | tf_op jit(solution)/shard_map/ppermute | solution.py:650
  232.0 4.9 %collective-permute-start.41 = (f32[40,768]{1,0:T(8,128)S(1)}, f32[40,768]{1,0:T(8,128)S(1)}, u32[]{:S(2)}, u32[]{:S(2)}) collective-permute-start(f32[40,768]{1,0:T(8,128)S(1)} %pad_maximum_fusion.11), channel_id=1, source_target_pairs={{0,2},{1,3},{2,0},{3,1},{4,6},{5,7},{6,4},{7,5},{8,10},{9,11},{10,... | collective-permute-start | bytes 368648 | tf_op jit(solution)/shard_map/ppermute | solution.py:650
  250.4 7.4 %collective-permute-start.49 = (f32[56,768]{1,0:T(8,128)S(1)}, f32[56,768]{1,0:T(8,128)S(1)}, u32[]{:S(2)}, u32[]{:S(2)}) collective-permute-start(f32[56,768]{1,0:T(8,128)S(1)} %pad_maximum_fusion.10), channel_id=1, source_target_pairs={{0,4},{4,0},{8,12},{12,8},{16,20},{20,16},{24,28},{28,24},{1,5},{5... | collective-permute-start | bytes 516104 | tf_op jit(solution)/shard_map/ppermute | solution.py:650
  251.3 10.0 %collective-permute-start.48 = (bf16[192,768]{1,0:T(8,128)(2,1)S(1)}, bf16[192,768]{1,0:T(8,128)(2,1)S(1)}, u32[]{:S(2)}, u32[]{:S(2)}) collective-permute-start(bf16[192,768]{1,0:T(8,128)(2,1)S(1)} %pad_maximum_fusion.6), channel_id=1, source_target_pairs={{0,4},{4,0},{8,12},{12,8},{16,20},{20,16},{24,28},{28,24},{1,5},{5... | collective-permute-start | bytes 884744 | tf_op jit(solution)/shard_map/ppermute | solution.py:650
  252.6 9.9 %collective-permute-start.47 = (bf16[192,768]{1,0:T(8,128)(2,1)S(1)}, bf16[192,768]{1,0:T(8,128)(2,1)S(1)}, u32[]{:S(2)}, u32[]{:S(2)}) collective-permute-start(bf16[192,768]{1,0:T(8,128)(2,1)S(1)} %pad_maximum_fusion.5), channel_id=1, source_target_pairs={{0,8},{4,12},{8,0},{12,4},{16,24},{20,28},{24,16},{28,20},{1,9},{5... | collective-permute-start | bytes 884744 | tf_op jit(solution)/shard_map/ppermute | solution.py:650
  252.9 7.3 %collective-permute-start.46 = (bf16[96,768]{1,0:T(8,128)(2,1)S(1)}, bf16[96,768]{1,0:T(8,128)(2,1)S(1)}, u32[]{:S(2)}, u32[]{:S(2)}) collective-permute-start(bf16[96,768]{1,0:T(8,128)(2,1)S(1)} %dynamic-slice_convert_fusion), channel_id=1, source_target_pairs={{0,16},{4,20},{8,24},{12,28},{16,0},{20,4},{24,8},{28,12},{1,17},{... | collective-permute-start | bytes 442376 | tf_op jit(solution)/shard_map/ppermute | solution.py:650
  262.6 13.9 %collective-permute-start.53 = (f32[88,768]{1,0:T(8,128)S(1)}, f32[88,768]{1,0:T(8,128)S(1)}, u32[]{:S(2)}, u32[]{:S(2)}) collective-permute-start(f32[88,768]{1,0:T(8,128)S(1)} %pad_maximum_fusion.8), channel_id=1, source_target_pairs={{0,8},{4,12},{8,0},{12,4},{16,24},{20,28},{24,16},{28,20},{1,9},{5... | collective-permute-start | bytes 811016 | tf_op jit(solution)/shard_map/ppermute | solution.py:650
  266.1 21.2 %collective-permute-start.52 = (bf16[384,768]{1,0:T(8,128)(2,1)S(1)}, bf16[384,768]{1,0:T(8,128)(2,1)S(1)}, u32[]{:S(2)}, u32[]{:S(2)}) collective-permute-start(bf16[384,768]{1,0:T(8,128)(2,1)S(1)} %pad_maximum_fusion.2.refs_3_), channel_id=1, source_target_pairs={{0,8},{4,12},{8,0},{12,4},{16,24},{20,28},{24,16},{28,20},{1,9},{5... | collective-permute-start | bytes 1769480 | tf_op jit(solution)/shard_map/ppermute | solution.py:650
  266.2 21.0 %collective-permute-start.51 = (bf16[384,768]{1,0:T(8,128)(2,1)S(1)}, bf16[384,768]{1,0:T(8,128)(2,1)S(1)}, u32[]{:S(2)}, u32[]{:S(2)}) collective-permute-start(bf16[384,768]{1,0:T(8,128)(2,1)S(1)} %pad_maximum_fusion.1.refs_1_), channel_id=1, source_target_pairs={{0,4},{4,0},{8,12},{12,8},{16,20},{20,16},{24,28},{28,24},{1,5},{5... | collective-permute-start | bytes 1769480 | tf_op jit(solution)/shard_map/ppermute | solution.py:650
  267.6 18.9 %collective-permute-start.50 = (bf16[96,768]{1,0:T(8,128)(2,1)S(1)}, bf16[96,768]{1,0:T(8,128)(2,1)S(1)}, u32[]{:S(2)}, u32[]{:S(2)}) collective-permute-start(bf16[96,768]{1,0:T(8,128)(2,1)S(1)} %add_convert_fusion.1), channel_id=1, source_target_pairs={{0,16},{4,20},{8,24},{12,28},{16,0},{20,4},{24,8},{28,12},{1,17},{... | collective-permute-start | bytes 442376 | tf_op jit(solution)/shard_map/ppermute | solution.py:650
  287.3 21.9 %collective-permute-start.54 = (f32[152,768]{1,0:T(8,128)S(1)}, f32[152,768]{1,0:T(8,128)S(1)}, u32[]{:S(2)}, u32[]{:S(2)}) collective-permute-start(f32[152,768]{1,0:T(8,128)S(1)} %pad_maximum_fusion.3), channel_id=1, source_target_pairs={{0,16},{4,20},{8,24},{12,28},{16,0},{20,4},{24,8},{28,12},{1,17},{... | collective-permute-start | bytes 1400840 | tf_op jit(solution)/shard_map/ppermute | solution.py:650
  290.1 23.7 %collective-permute-start.55 = (bf16[192,768]{1,0:T(8,128)(2,1)S(1)}, bf16[192,768]{1,0:T(8,128)(2,1)S(1)}, u32[]{:S(2)}, u32[]{:S(2)}) collective-permute-start(bf16[192,768]{1,0:T(8,128)(2,1)S(1)} %pad_maximum_fusion.7.refs_5_), channel_id=1, source_target_pairs={{0,4},{4,0},{8,12},{12,8},{16,20},{20,16},{24,28},{28,24},{1,5},{5... | collective-permute-start | bytes 884744 | tf_op jit(solution)/shard_map/ppermute | solution.py:650
  291.4 22.4 %collective-permute-start.56 = (bf16[192,768]{1,0:T(8,128)(2,1)S(1)}, bf16[192,768]{1,0:T(8,128)(2,1)}, u32[]{:S(2)}, u32[]{:S(2)}) collective-permute-start(bf16[192,768]{1,0:T(8,128)(2,1)S(1)} %pad_maximum_fusion.7.refs_5_), channel_id=1, source_target_pairs={{0,8},{4,12},{8,0},{12,4},{16,24},{20,28},{24,16},{28,20},{1,9},{5... | collective-permute-start | bytes 884744 | tf_op jit(solution)/shard_map/ppermute | solution.py:650
  292.1 21.6 %collective-permute-start.57 = (bf16[192,768]{1,0:T(8,128)(2,1)S(1)}, bf16[192,768]{1,0:T(8,128)(2,1)}, u32[]{:S(2)}, u32[]{:S(2)}) collective-permute-start(bf16[192,768]{1,0:T(8,128)(2,1)S(1)} %pad_maximum_fusion.7.refs_5_), channel_id=1, source_target_pairs={{0,12},{4,8},{8,4},{12,0},{16,28},{20,24},{24,20},{28,16},{1,13},{... | collective-permute-start | bytes 884744 | tf_op jit(solution)/shard_map/ppermute | solution.py:650
  (58 other events, 289.5 us)
